TPU v7x, 256 devices: a whole 4x4x8 slice. The times are simulated.
256 devices in a mesh: horiz: 32 (over x, z), lev: 8 (over y, core).
Axes of the slice: x: 4, y: 4, z: 8, core: 2. Of those that a mesh axis runs over, the one named last changes fastest.
Arguments:
- perturb: bfloat16 [16, 256, 16384], P('lev', None, 'horiz'), may hold values from -6 to 6
- mean_state: float32 [16, 16384], P('lev', 'horiz'), may hold values from -6 to 6
- obs_value: float32 [2, 1024], replicated, may hold values from -8 to 8
- obs_var: float32 [2, 1024], replicated, may hold values from 0.3 to 3
- obs_weight: float32 [2, 1024], replicated, may hold values from 0 to 1
- obs_tile: int32 [2, 1024], replicated, may hold values from 0 to 31, as said below
- obs_col: int32 [2, 1024], replicated, may hold values from 0 to 511
- obs_level: int32 [2, 1024], replicated, may hold values from 0 to 15
- loc_horiz: float32 [2, 32, 1024], replicated, may hold values from 0.2 to 1
- loc_vert: float32 [2, 16, 1024], replicated, may hold values from 0.2 to 1
Outputs:
- perturb_out: bfloat16 [16, 256, 16384], P('lev', None, 'horiz')
- mean_out: float32 [16, 16384], P('lev', 'horiz')
Inputs may be any that keep to these rules, and one draw needn't show every extreme that they name: `obs_tile`: in each batch every tile holds the site of at least one observation at its last column.
All inputs are finite; a program needn't handle non-finite values.
Results may differ from a plain program's by a relative error of at most 0.0051.
Values sent between devices are 32-bit elements; how exact they have to be, the bound alone decides.
A program may use at most 128 MiB of HBM per device.

v0:
```python
import jax
import jax.numpy as jnp
from jax import lax
from jax.sharding import PartitionSpec as P


def shifted_2(array, axis, by):
    peers = lax.axis_size(axis)
    return lax.ppermute(array, axis, [(i, (i + by) % peers) for i in range(peers)])


def extend_state(perturb, mean_state):
    edge_col = shifted_2((perturb[:, :, 0].astype(jnp.float32), mean_state[:, 0]), "horiz", -1)
    widened = jnp.concatenate([perturb.astype(jnp.float32), edge_col[0][:, :, None]], axis=2)
    stacked = jnp.moveaxis(widened, 1, 0).reshape(widened.shape[1], -1)
    mean_cells = jnp.concatenate([mean_state, edge_col[1][:, None]], axis=1).reshape(-1)
    return (stacked, mean_cells)


def pick_sites(stacked, mean_cells, site_tiles, site_cols, levels, fraction, lev_count, col_count):
    my_tile = lax.axis_index("horiz")
    first_level = lax.axis_index("lev") * lev_count
    is_owned = (
        (site_tiles == my_tile) & (levels >= first_level) & (levels < first_level + lev_count)
    )
    position = jnp.where(is_owned, (levels - first_level) * (col_count + 1) + site_cols, 0)
    left_vals = stacked[:, position]
    right_vals = stacked[:, position + 1]
    site_rows = jnp.where(
        is_owned[None, :],
        (1.0 - fraction)[None, :] * left_vals + fraction[None, :] * right_vals,
        0.0,
    )
    site_means = jnp.where(
        is_owned, (1.0 - fraction) * mean_cells[position] + fraction * mean_cells[position + 1], 0.0
    )
    return (site_rows, site_means)


def solve_batch(panel_rows, site_means, value_row, var_row, members):
    innovation = value_row - site_means
    innov_cov = jnp.dot(panel_rows, panel_rows.T, precision=lax.Precision.HIGHEST) / (
        members - 1
    ) + jnp.diag(var_row)
    factor = jnp.linalg.cholesky(innov_cov)
    half_solve = lax.linalg.triangular_solve(
        factor, innovation[:, None], left_side=True, lower=True
    )
    weights = lax.linalg.triangular_solve(
        factor, half_solve, left_side=True, lower=True, transpose_a=True
    )[:, 0]
    shifted = factor + jnp.diag(jnp.sqrt(var_row))
    left_solve = lax.linalg.triangular_solve(shifted, panel_rows, left_side=True, lower=True)
    gain_rows = lax.linalg.triangular_solve(
        factor, left_solve, left_side=True, lower=True, transpose_a=True
    )
    return (weights, gain_rows)


def update_tiles(
    perturb, mean_state, rows_half, gain_half, weights, horiz_weight, vert_table, first_level
):
    lev_count, members, col_count = perturb.shape
    new_slabs = []
    new_means = []
    for level_no in range(lev_count):
        vert_weight = lax.dynamic_index_in_dim(
            vert_table, first_level + level_no, 0, keepdims=False
        )
        slab_rows = perturb[level_no]
        spread = lax.dot_general(
            slab_rows, rows_half, (((0,), (0,)), ((), ())), preferred_element_type=jnp.float32
        ) / (members - 1)
        damping = horiz_weight * vert_weight
        damped = spread * damping[None, :]
        tile_gain = damped.astype(jnp.bfloat16)
        new_means.append(
            mean_state[level_no] + jnp.dot(damped, weights, precision=lax.Precision.HIGHEST)
        )
        increment = lax.dot_general(
            gain_half, tile_gain, (((1,), (1,)), ((), ())), preferred_element_type=jnp.float32
        )
        new_slabs.append((slab_rows.astype(jnp.float32) - increment).astype(jnp.bfloat16))
    return (jnp.stack(new_slabs), jnp.stack(new_means))


def shards(
    perturb,
    mean_state,
    obs_value,
    obs_var,
    obs_weight,
    obs_tile,
    obs_col,
    obs_level,
    loc_horiz,
    loc_vert,
):
    lev_count, members, col_count = perturb.shape
    batch_count = obs_tile.shape[0]
    my_tile = lax.axis_index("horiz")
    first_level = lax.axis_index("lev") * lev_count
    for batch_no in range(batch_count):
        stacked, mean_cells = extend_state(perturb, mean_state)
        site_rows, site_means = pick_sites(
            stacked,
            mean_cells,
            obs_tile[batch_no],
            obs_col[batch_no],
            obs_level[batch_no],
            obs_weight[batch_no],
            lev_count,
            col_count,
        )
        obs_rows, obs_means = lax.psum((site_rows, site_means), ("horiz", "lev"))
        weights, gain_rows = solve_batch(
            obs_rows.T, obs_means, obs_value[batch_no], obs_var[batch_no], members
        )
        horiz_weight = lax.dynamic_index_in_dim(loc_horiz[batch_no], my_tile, 0, keepdims=False)
        perturb, mean_state = update_tiles(
            perturb,
            mean_state,
            obs_rows.astype(jnp.bfloat16),
            gain_rows.T.astype(jnp.bfloat16),
            weights,
            horiz_weight,
            loc_vert[batch_no],
            first_level,
        )
    return (perturb, mean_state)


def solution(mesh):
    return jax.shard_map(
        shards,
        mesh=mesh,
        in_specs=(
            P("lev", None, "horiz"),
            P("lev", "horiz"),
            P(),
            P(),
            P(),
            P(),
            P(),
            P(),
            P(),
            P(),
        ),
        out_specs=(P("lev", None, "horiz"), P("lev", "horiz")),
        check_vma=False,
    )
```

profile of v0, /device:TPU:1, one launch (start us, length us, event | category | flops | bytes accessed | tf_op | source)
XLA Modules:
  0.0 1556.4 jit_solution(2162338668681742042)
XLA Ops:
  8.2 8.7 collective-permute-start
  27.2 3.5 gather_fusion
  30.7 3.5 gather_fusion.1
  35.9 6.1 gather_fusion.5
  42.1 6.2 gather_fusion.4
  48.3 75.4 %psum.30 = f32[1024]{0:T(1024)S(1)} all-reduce(f32[1024]{0:T(1024)S(1)} %add_select_fusion.1), channel_id=1, replica_groups=mesh['horiz'=32,'lev'=8] {'horiz','lev'}, use_global_device_ids=true, to_apply=%region_18.22 | all-reduce | flops 1024 | bytes 8192 | tf_op jit(solution)/shard_map/psum | solution.py:115
  123.7 162.5 %all-reduce.4.cloned.1.call-done = f32[256,1024]{0,1:T(8,128)} async-done(((f32[256,1024]{0,1:T(8,128)}), f32[256,1024]{0,1:T(8,128)}) %all-reduce.4.cloned.1.call-update) | async-done | bytes 1048592 | tf_op jit(solution)/shard_map/psum | solution.py:115
  286.2 7.2 select_add_fusion.1
  293.4 5.5 copy.108
  298.9 4.4 fusion.1
  305.3 11.7 cholesky.619
  317.0 9.8 custom-call.67
  330.0 11.7 cholesky.638
  342.3 9.8 custom-call.68
  357.6 11.7 cholesky.659
  370.1 9.8 custom-call.69
  381.2 3.5 convolution_subtract_fusion.9
  384.7 11.7 cholesky.678
  397.2 9.8 custom-call.70
  411.3 11.8 cholesky.697
  424.0 9.8 custom-call.71
  434.9 3.2 convolution_subtract_fusion.13
  438.1 11.7 cholesky.716
  450.6 9.8 custom-call.72
  464.4 11.7 cholesky.735
  476.8 9.8 custom-call.73
  489.8 11.7 cholesky.752
  512.2 6.7 fusion.6
  519.4 23.5 %while.17 = (s32[]{:T(128)}, f32[1024,1024]{0,1:T(8,128)}, s32[8,2]{0,1:T(2,128)S(1)}, f32[8,128,128]{2,1,0:T(8,128)S(1)}, s32[]{:T(128)}) while((s32[]{:T(128)}, f32[1024,1024]{0,1:T(8,128)}, s32[8,2]{0,1:T(2,128)S(1)}, f32[8,128,128]{2,1,0:T(8,128)S(1)}, s32[]{:T(128)}) %tuple.235), condition=%wide.while_cond.1, body=%wide.while_body.1.sunk | while | flops 2 | bytes 393321 | solution.py:54
  542.9 78.6 %custom-call.75 = f32[8,128,128]{1,2,0:T(8,128)S(1)} custom-call(f32[8,128,128]{2,1,0:T(8,128)S(1)} %get-tuple-element.64), custom_call_target="InvertDiagBlocksLowerTriangular" | custom-call | tf_op jit(solution)/shard_map/triangular_solve/custom-call.16 | solution.py:54
  642.5 23.5 %while.16 = (s32[]{:T(128)}, f32[1024,1024]{0,1:T(8,128)}, s32[8,2]{0,1:T(2,128)S(1)}, f32[8,128,128]{2,1,0:T(8,128)S(1)}, s32[]{:T(128)}) while((s32[]{:T(128)}, f32[1024,1024]{0,1:T(8,128)}, s32[8,2]{0,1:T(2,128)S(1)}, f32[8,128,128]{2,1,0:T(8,128)S(1)}, s32[]{:T(128)}) %tuple.248), condition=%wide.while_cond, body=%wide.while_body.sunk | while | flops 2 | bytes 393321 | solution.py:53
  666.0 78.8 %custom-call.74 = f32[8,128,128]{1,2,0:T(8,128)S(1)} custom-call(f32[8,128,128]{2,1,0:T(8,128)S(1)} %get-tuple-element.63), custom_call_target="InvertDiagBlocksLowerTriangular" | custom-call | tf_op jit(solution)/shard_map/triangular_solve/custom-call.7 | solution.py:53
  774.3 5.3 collective-permute-start.1
  787.3 4.7 gather_fusion.2
  792.0 4.7 gather_fusion.3
  801.2 5.1 collective-permute-start.3
  807.2 6.1 gather_fusion.6
  813.3 6.2 gather_fusion.7
  819.5 77.6 %psum.31 = f32[1024]{0:T(1024)S(1)} all-reduce(f32[1024]{0:T(1024)S(1)} %add_select_fusion), channel_id=1, replica_groups=mesh['horiz'=32,'lev'=8] {'horiz','lev'}, use_global_device_ids=true, to_apply=%region_19.25 | all-reduce | flops 1024 | bytes 8192 | tf_op jit(solution)/shard_map/psum | solution.py:115
  897.1 155.1 %all-reduce.6.cloned.1.call-done = f32[256,1024]{0,1:T(8,128)} async-done(((f32[256,1024]{0,1:T(8,128)}), f32[256,1024]{0,1:T(8,128)}) %all-reduce.6.cloned.1.call-update) | async-done | bytes 1048592 | tf_op jit(solution)/shard_map/psum | solution.py:115
  1052.3 7.2 select_add_fusion
  1059.5 5.7 copy.129
  1065.2 4.4 fusion
  1071.6 11.7 cholesky.767
  1083.3 9.8 custom-call.76
  1096.3 11.7 cholesky.786
  1108.6 9.8 custom-call.77
  1123.9 11.7 cholesky.807
  1136.4 9.8 custom-call.78
  1147.4 3.3 convolution_subtract_fusion.8
  1150.8 11.7 cholesky.826
  1163.3 9.8 custom-call.79
  1177.4 12.1 cholesky.845
  1190.3 9.8 custom-call.80
  1204.4 11.7 cholesky.864
  1216.9 9.8 custom-call.81
  1230.6 11.7 cholesky.883
  1243.1 9.8 custom-call.82
  1256.1 11.7 cholesky.900
  1278.9 6.7 fusion.3
  1285.6 24.3 %while.19 = (s32[]{:T(128)}, f32[1024,1024]{0,1:T(8,128)}, s32[8,2]{0,1:T(2,128)S(1)}, f32[8,128,128]{2,1,0:T(8,128)S(1)}, s32[]{:T(128)}) while((s32[]{:T(128)}, f32[1024,1024]{0,1:T(8,128)}, s32[8,2]{0,1:T(2,128)S(1)}, f32[8,128,128]{2,1,0:T(8,128)S(1)}, s32[]{:T(128)}) %tuple.249), condition=%wide.while_cond.1.clone, body=%wide.while_body.1.clone.sunk | while | flops 2 | bytes 393321 | solution.py:54
  1309.9 78.6 %custom-call.84 = f32[8,128,128]{1,2,0:T(8,128)S(1)} custom-call(f32[8,128,128]{2,1,0:T(8,128)S(1)} %get-tuple-element.66), custom_call_target="InvertDiagBlocksLowerTriangular" | custom-call | tf_op jit(solution)/shard_map/triangular_solve/custom-call.16 | solution.py:54
  1409.6 24.1 %while.18 = (s32[]{:T(128)}, f32[1024,1024]{0,1:T(8,128)}, s32[8,2]{0,1:T(2,128)S(1)}, f32[8,128,128]{2,1,0:T(8,128)S(1)}, s32[]{:T(128)}) while((s32[]{:T(128)}, f32[1024,1024]{0,1:T(8,128)}, s32[8,2]{0,1:T(2,128)S(1)}, f32[8,128,128]{2,1,0:T(8,128)S(1)}, s32[]{:T(128)}) %tuple.250), condition=%wide.while_cond.clone, body=%wide.while_body.clone.sunk | while | flops 2 | bytes 393321 | solution.py:53
  1433.7 79.5 %custom-call.83 = f32[8,128,128]{1,2,0:T(8,128)} custom-call(f32[8,128,128]{2,1,0:T(8,128)S(1)} %get-tuple-element.65), custom_call_target="InvertDiagBlocksLowerTriangular" | custom-call | tf_op jit(solution)/shard_map/triangular_solve/custom-call.7 | solution.py:53
  (572 shorter events, 298.9 us)
Async XLA Ops:
  7.2 279.0 %all-reduce.4.cloned.1.call-start = ((), (), s32[]{:S(2)}) async-start(), calls=%async_computation | async-start | bytes 2097152 | tf_op jit(solution)/shard_map/psum | solution.py:115
  8.2 18.3 %collective-permute-start = (f32[2,256]{1,0:T(2,128)S(1)}, f32[2,256]{1,0:T(2,128)S(1)}, u32[]{:S(2)}, u32[]{:S(2)}) collective-permute-start(f32[2,256]{1,0:T(2,128)S(1)} %convert_reduce_fusion.1), channel_id=1, source_target_pairs={{0,248},{8,0},{16,8},{24,16},{32,24},{40,32},{48,40},{56,48},{64,5... | collective-permute-start | bytes 6152 | tf_op jit(solution)/shard_map/ppermute | solution.py:9
  17.7 18.0 %collective-permute-start.2 = (f32[2]{0:T(128)S(1)}, f32[2]{0:T(128)S(1)}, u32[]{:S(2)}, u32[]{:S(2)}) collective-permute-start(f32[2]{0:T(128)S(1)} %slice_reduce_fusion), channel_id=1, source_target_pairs={{0,248},{8,0},{16,8},{24,16},{32,24},{40,32},{48,40},{56,48},{64,5... | collective-permute-start | bytes 32 | tf_op jit(solution)/shard_map/ppermute | solution.py:9
  34.2 1.7 copy-start.10
  35.7 1016.6 %all-reduce.6.cloned.1.call-start = ((), (), s32[]{:S(2)}) async-start(), calls=%async_computation.1 | async-start | bytes 2097152 | tf_op jit(solution)/shard_map/psum | solution.py:115
  303.4 1.9 copy-start.4
  353.2 2.0 copy-start
  542.9 201.9 %copy-start.3 = (f32[256,1024]{0,1:T(8,128)S(1)}, f32[256,1024]{0,1:T(8,128)}, u32[]{:S(2)}) copy-start(f32[256,1024]{0,1:T(8,128)} %all-reduce.4.cloned.1.call-done) | copy-start | bytes 3145732
  766.5 4.1 copy-start.8
  773.2 6.5 copy-start.6
  774.3 6.0 collective-permute-start.1
  801.2 5.8 collective-permute-start.3
  1069.7 1.9 copy-start.5
  1119.5 2.0 copy-start.1
  1309.9 203.2 %copy-start.2 = (f32[256,1024]{0,1:T(8,128)S(1)}, f32[256,1024]{0,1:T(8,128)}, u32[]{:S(2)}) copy-start(f32[256,1024]{0,1:T(8,128)} %all-reduce.6.cloned.1.call-done) | copy-start | bytes 3145732
  1513.2 7.4 copy-start.9
  1537.4 4.1 copy-start.7
Sparse Core Ops, SparseCore 0:
  35.8 250.3 all-reduce.3
  799.9 252.3 all-reduce.5
where the time goes:
time: 1570 us; the launch traced here: 1560 us
  other arithmetic  687 us (44%)
  waiting for transfers between devices  319 us (20%)
  local copies, waits for them, and re-layouts  177 us (11%)
  matrix products  172 us (11%)
  blocking collectives  153 us (10%)
  between operations  27.1 us (2%)
  starting transfers between devices  19.9 us (1%)
    another operation x62, other arithmetic, solve_batch(): factor = jnp.linalg.cholesky(innov_cov)  336 us
    psum x2, waiting for transfers between devices, shards(): obs_rows, obs_means = lax.psum((site_rows, site_means), ('horiz', 'lev'))  318 us
    another operation x5, other arithmetic, solve_batch(): lax.linalg.triangular_solve(factor, left_solve, left_side=True, lower=Tru...  171 us
    another operation x2, other arithmetic, solve_batch(): lax.linalg.triangular_solve(shifted, panel_rows, left_side=True, lower=True)  158 us
    psum x2, blocking collectives, shards(): obs_rows, obs_means = lax.psum((site_rows, site_means), ('horiz', 'lev'))  153 us
    another operation x28, matrix products, solve_batch(): factor = jnp.linalg.cholesky(innov_cov)  52.6 us
    another operation x93, local copies, waits for them, and re-layouts, solve_batch(): lax.linalg.triangular_solve(factor, left_solve, left_side=True, lower=Tru...  47.3 us
    another operation x80, local copies, waits for them, and re-layouts, solve_batch(): lax.linalg.triangular_solve(shifted, panel_rows, left_side=True, lower=True)  47.1 us
  transfers between devices with their start and end apart: 6, of which 4 were waited for; matrix products, arithmetic and copies ran while one was open for 3% of the time, Pallas kernels for 0%

commit v1 on v0

v1 whole, which is shorter than its diff:
```python
import functools
import jax
import jax.numpy as jnp
from jax import lax
from jax.experimental import pallas as pl
from jax.experimental.pallas import tpu as pltpu
from jax.sharding import PartitionSpec as P

F32 = jnp.float32
BF16 = jnp.bfloat16
HIGHEST = lax.Precision.HIGHEST
MESH = pl.DeviceIdType.MESH
B = 128
Q = 32
NT = ((1,), (1,))
TN = ((0,), (0,))
NN = ((1,), (0,))


def mm(a, b, dims=NN):
    return lax.dot_general(a, b, (dims, ((), ())), precision=HIGHEST, preferred_element_type=F32)


def mm16(a, b):
    return jnp.dot(a, b, preferred_element_type=F32)


def columns_of(rows):
    return jnp.concatenate([rows] * 16, axis=0).T


def rows_at(i):
    return pl.ds(pl.multiple_of(i * B, B), B)


def gather_sites(batch, x_ref, xm_ref, tile_ref, col_ref, level_ref, frac_ref, out_ref):
    levels, members, cols = x_ref.shape
    tiles = 32
    my_tile = lax.axis_index("horiz")
    first = lax.axis_index("lev") * levels
    row = lax.broadcasted_iota(jnp.int32, (8, B), 0)
    width = 2 * B
    cells = lax.broadcasted_iota(jnp.int32, (cols, width), 0)
    parts = []
    for lev in range(levels):
        xm = xm_ref[lev : lev + 1, :]
        hi = xm.astype(BF16).astype(F32)
        mid = (xm - hi).astype(BF16).astype(F32)
        low = xm - hi - mid
        r16 = lax.broadcasted_iota(jnp.int32, (16, cols), 0)
        stack = jnp.where(r16 == 0, hi, jnp.where(r16 == 1, mid, jnp.where(r16 == 2, low, 0.0)))
        parts.append(stack.astype(BF16))
    for jb in range(4):
        lanes = slice(jb * width, (jb + 1) * width)
        tile = tile_ref[batch : batch + 1, lanes]
        col = col_ref[batch : batch + 1, lanes]
        level = level_ref[batch : batch + 1, lanes]
        frac = frac_ref[batch : batch + 1, lanes]
        wraps = col == cols - 1
        next_tile = jnp.where(wraps, jnp.where(tile == tiles - 1, 0, tile + 1), tile)
        next_col = jnp.where(wraps, 0, col + 1)
        vals = []
        for t, c in ((tile, col), (next_tile, next_col)):
            v = jnp.zeros((members, width), F32)
            m = jnp.zeros((16, width), F32)
            for lev in range(levels):
                pos = jnp.where((t == my_tile) & (level == first + lev), c, -1)
                hot = jnp.where(cells == pos, 1.0, 0.0).astype(BF16)
                v = v + mm16(x_ref[lev], hot)
                m = m + mm16(parts[lev], hot)
            vals.append((v, jnp.sum(m[0:8], axis=0, keepdims=True)))
        site = (1.0 - frac) * vals[0][0] + frac * vals[1][0]
        mean = (1.0 - frac) * vals[0][1] + frac * vals[1][1]
        for core in range(2):
            half = slice(core * B, (core + 1) * B)
            out_ref[core, jb, 0:32] = site[:, half].reshape(32, 8, B)
            out_ref[core, jb, 32] = jnp.where(row == 0, mean[:, half], 0.0)


def gather_kernel(x_ref, xm_ref, tile_ref, col_ref, level_ref, frac_ref, out_ref):
    gather_sites(0, x_ref, xm_ref, tile_ref, col_ref, level_ref, frac_ref, out_ref)


def sum_kernel(c_ref, o_ref, r0, a0, r1, a1, r2, a2, r3, a3, send, recv):
    horiz = lax.axis_index("horiz")
    lev = lax.axis_index("lev")
    x, z = horiz // 8, horiz % 8
    y, core = lev // 2, lev % 2

    def at(dx=0, dz=0, dy=0, dc=0):
        return (((x + dx) % 4) * 8 + (z + dz) % 8, ((y + dy) % 4) * 2 + (core + dc) % 2)

    peers = (
        [at(dc=1)]
        + [at(dy=k) for k in range(1, 4)]
        + [at(dx=k) for k in range(1, 4)]
        + [at(dz=k) for k in range(1, 8)]
    )
    barrier = pltpu.get_barrier_semaphore()
    for peer in peers:
        pl.semaphore_signal(barrier, inc=1, device_id=peer, device_id_type=MESH)
    pl.semaphore_wait(barrier, len(peers))

    count = [0]

    def start(src, dst, peer):
        k = count[0]
        count[0] += 1
        copy = pltpu.make_async_remote_copy(
            src_ref=src, dst_ref=dst, send_sem=send.at[k], recv_sem=recv.at[k],
            device_id=peer, device_id_type=MESH,
        )
        copy.start()
        return copy

    sent = []
    other = 1 - core
    first = []
    for k in (1, 2, 3, 0):
        yk = (y + k) % 4
        first.append((yk, start(c_ref.at[other, yk], r0.at[yk], at(dc=1))))
    ys = []
    for k, (yk, copy) in zip((1, 2, 3, 0), first):
        copy.wait_recv()
        a0[yk] = c_ref[core, yk] + r0[yk]
        if k:
            ys.append(start(a0.at[yk], r1.at[k - 1], at(dy=k)))
    sent += [copy for _, copy in first]
    for copy in ys:
        copy.wait_recv()
    a1[...] = (a0[y] + r1[0]) + (r1[1] + r1[2])
    sent += ys
    xs = []
    for k in range(1, 4):
        xk = (x + k) % 4
        xs.append(start(a1.at[pl.ds(8 * xk, 8)], r2.at[k - 1, pl.ds(0, 8)], at(dx=k)))
        xs.append(start(a1.at[pl.ds(32, 1)], r2.at[k - 1, pl.ds(8, 1)], at(dx=k)))
    for copy in xs:
        copy.wait_recv()
    a2[0:8] = (a1[pl.ds(8 * x, 8)] + r2[0, 0:8]) + (r2[1, 0:8] + r2[2, 0:8])
    a2[8:9] = (a1[32:33] + r2[0, 8:9]) + (r2[1, 8:9] + r2[2, 8:9])
    sent += xs
    zs = []
    for k in range(1, 8):
        zk = (z + k) % 8
        zs.append(start(a2.at[pl.ds(zk, 1)], r3.at[k - 1, pl.ds(0, 1)], at(dz=k)))
        zs.append(start(a2.at[pl.ds(8, 1)], r3.at[k - 1, pl.ds(1, 1)], at(dz=k)))
    for copy in zs:
        copy.wait_recv()
    mine = a2[z]
    mean = a2[8]
    for k in range(7):
        mine = mine + r3[k, 0]
        mean = mean + r3[k, 1]
    o_ref[core, y, 8 * x + z] = mine
    o_ref[core, y, 32] = mean
    sent += zs
    zs = []
    for k in range(1, 8):
        spot = o_ref.at[core, y, pl.ds(8 * x + z, 1)]
        zs.append(start(spot, spot, at(dz=k)))
    for copy in zs:
        copy.wait_recv()
    xs = []
    for k in range(1, 4):
        spot = o_ref.at[core, y, pl.ds(8 * x, 8)]
        xs.append(start(spot, spot, at(dx=k)))
    for copy in xs:
        copy.wait_recv()
    spot = o_ref.at[core, y]
    ys = [start(spot, spot, at(dy=k)) for k in range(1, 4)]
    cs = [start(spot, spot, at(dc=1))]
    for k, copy in zip(range(1, 4), ys):
        copy.wait_recv()
        spot = o_ref.at[core, (y - k + 4) % 4]
        cs.append(start(spot, spot, at(dc=1)))
    for copy in cs:
        copy.wait_recv()
    for copy in sent + zs + xs + ys + cs:
        copy.wait_send()


COPIES = 4 + 3 + 6 + 14 + 7 + 3 + 3 + 4


def sum_over_devices(share):
    vm = pl.BlockSpec(memory_space=pltpu.VMEM)

    def buf(*shape):
        return pltpu.VMEM(shape + (8, B), F32)

    return pl.pallas_call(
        sum_kernel,
        out_shape=jax.ShapeDtypeStruct(share.shape, F32),
        in_specs=[vm],
        out_specs=vm,
        scratch_shapes=[
            buf(4, 33), buf(4, 33), buf(3, 33), buf(33), buf(3, 9), buf(9), buf(7, 2), buf(2),
            pltpu.SemaphoreType.DMA((COPIES,)),
            pltpu.SemaphoreType.DMA((COPIES,)),
        ],
        compiler_params=pltpu.CompilerParams(
            collective_id=0, has_side_effects=True, vmem_limit_bytes=24 * 2**20
        ),
    )(share)


def factor_block(s, dcol):
    nt = Q // 8
    row = lax.broadcasted_iota(jnp.int32, (8, B), 0)
    eye = jnp.where(
        lax.broadcasted_iota(jnp.int32, (B, B), 0) == lax.broadcasted_iota(jnp.int32, (B, B), 1),
        1.0,
        0.0,
    )
    m, a, z = s, eye, eye
    out_a, out_z = [], []
    for o in range(0, B, Q):
        w_t = [m[8 * t : 8 * t + 8] for t in range(nt)]
        a_t = [a[8 * t : 8 * t + 8] for t in range(nt)]
        z_t = [z[8 * t : 8 * t + 8] for t in range(nt)]
        cols = [
            [
                None if t < c // 8 else jnp.broadcast_to(w_t[t][:, o + c : o + c + 1], (8, B))
                for t in range(nt)
            ]
            for c in range(Q)
        ]
        for r in range(Q):
            tr, rr = r // 8, r % 8
            p = cols[r][tr][rr : rr + 1]
            rs = lax.rsqrt(p)
            l = [None if t < tr else cols[r][t] * rs for t in range(nt)]
            u = w_t[tr][rr : rr + 1] * rs
            av = a_t[tr][rr : rr + 1] * rs
            zv = z_t[tr][rr : rr + 1] / (p * rs + dcol[o + r : o + r + 1])
            for c in range(r + 1, Q):
                f = l[c // 8][c % 8 : c % 8 + 1]
                for t in range(c // 8, nt):
                    cols[c][t] = cols[c][t] - l[t] * f
            for t in range(tr, nt):
                lt = l[t] if t > tr else jnp.where(row > rr, l[t], 0.0)
                for rows, v in ((w_t, u), (a_t, av), (z_t, zv)):
                    new = rows[t] - lt * v
                    if t == tr:
                        new = jnp.where(row == rr, jnp.broadcast_to(v, (8, B)), new)
                    rows[t] = new
        u_b, a_b, z_b = (jnp.concatenate(rows, 0) for rows in (w_t, a_t, z_t))
        out_a.append(a_b)
        out_z.append(z_b)
        if o + Q < B:
            step = mm(u_b, jnp.concatenate([u_b, a_b, z_b], 1), TN)[o + Q :]
            m = m[Q:] - step[:, :B]
            a = a[Q:] - step[:, B : 2 * B]
            z = z[Q:] - step[:, 2 * B :]
    return jnp.concatenate(out_a, 0), jnp.concatenate(out_z, 0)


def analyse(
    panel_ref, x_ref, xm_ref, val_ref, var_ref, damp_ref, xo_ref, xmo_ref,
    a_ref, yb_ref, p_ref, qs_ref, s_ref, linv_ref, minv_ref, t1_ref, aq_ref, qv_ref, lz_ref,
    wl_ref, d_ref, vcol_ref, w_ref, gt_ref, k_ref,
):
    levels, members, cols = x_ref.shape
    n = a_ref.shape[0]
    nb = n // B
    c = 1.0 / (members - 1.0) ** 0.5

    def square(k):
        return lax.broadcasted_iota(jnp.int32, (k, k), 0) == lax.broadcasted_iota(
            jnp.int32, (k, k), 1
        )

    eye_m = jnp.where(square(members), 1.0, 0.0)
    diag = square(B)
    for i in range(nb):
        y_i = panel_ref[i % 2, i // 2, 0:32].reshape(members, B).T
        a_ref[i * B : (i + 1) * B] = y_i * c
        yb_ref[i * B : (i + 1) * B] = y_i.astype(BF16)
        d_ref[i : i + 1] = val_ref[i : i + 1] - panel_ref[i % 2, i // 2, 32][0:1]
    var_cols = columns_of(var_ref[...])
    for i in range(nb):
        vcol_ref[i] = jnp.broadcast_to(var_cols[:, i : i + 1], (B, B))
    p_ref[...] = eye_m
    qs_ref[0] = eye_m * (1.0 / c)
    a_0 = a_ref[0:B]
    s_ref[...] = mm(a_0, a_0, NT) + jnp.where(diag, var_ref[0:1], 0.0)
    for ref in (linv_ref, minv_ref, t1_ref, aq_ref, qv_ref):
        ref[...] = jnp.zeros_like(ref)

    def finish_previous(i):
        linv, minv, t1 = linv_ref[...], minv_ref[...], t1_ref[...]
        ip = jnp.maximum(i - 1, 0)
        v = mm(linv, t1)
        z = mm(minv, aq_ref[...])
        lz_ref[rows_at(i)] = mm(linv, z, TN)
        p = p_ref[...] - mm(v, v, TN)
        q = qs_ref[ip] - mm(v, z, TN)
        qv = qv_ref[...]
        rhs = d_ref[pl.ds(ip, 1)] - mm(qv, a_ref[rows_at(ip)], NT)
        qv = qv + mm(mm(rhs, linv, NT), v)
        return p, q, qv

    def step(i, carry):
        p, q, qv = finish_previous(i)
        i_next = jnp.minimum(i + 1, nb - 1)
        a_i = a_ref[rows_at(i)]
        a_n = a_ref[rows_at(i_next)]
        t1 = mm(a_i, p)
        t1_n = mm(a_n, p)
        s_nn = mm(t1_n, a_n, NT) + jnp.where(diag, var_ref[pl.ds(i_next, 1)], 0.0)
        s_ni = mm(t1_n, a_i, NT)
        aq = mm(a_i, q)
        linv, minv = factor_block(s_ref[...], jnp.sqrt(vcol_ref[i]))
        l_ni = mm(s_ni, linv, NT)
        s_ref[...] = s_nn - mm(l_ni, l_ni, NT)
        linv_ref[...] = linv
        minv_ref[...] = minv
        t1_ref[...] = t1
        aq_ref[...] = aq
        p_ref[...] = p
        qs_ref[i] = q
        qv_ref[...] = qv
        return carry

    lax.fori_loop(0, nb, step, 0)
    p, q, qv = finish_previous(nb)

    def over_obs(rows):
        total = jnp.zeros((8, members), F32)
        for i in range(nb):
            total = total + mm(jnp.broadcast_to(rows[i : i + 1], (8, B)), a_ref[i * B : (i + 1) * B])
        return total

    def times_a(v):
        return jnp.concatenate(
            [mm(v, a_ref[i * B : (i + 1) * B], NT)[0:1] for i in range(nb)], axis=0
        )

    d, var = d_ref[...], var_ref[...]
    w = (d - times_a(qv)) / var
    rest = d - var * w - times_a(over_obs(w))
    w = w + (rest - times_a(mm(over_obs(rest / var), p))) / var
    w_cols = columns_of(w)

    for i in range(nb):
        g = lz_ref[(i + 1) * B : (i + 2) * B]
        if i < nb - 1:
            inv = 1.0 / vcol_ref[i]
            g = g - mm(a_ref[i * B : (i + 1) * B], qs_ref[i + 1] - q) * jnp.concatenate([inv, inv], 1)
        gt_ref[:, i * B : (i + 1) * B] = g.T.astype(BF16)

    for lev in range(levels):
        damp_cols = columns_of(damp_ref[lev] * (1.0 / (members - 1.0)))
        slab = x_ref[lev]
        mean = jnp.zeros((8, cols), F32)
        for i in range(nb):
            f = mm16(yb_ref[i * B : (i + 1) * B], slab) * damp_cols[:, i : i + 1]
            k_ref[i * B : (i + 1) * B] = f.astype(BF16)
            mean = mean + jnp.sum((f * w_cols[:, i : i + 1]).reshape(B // 8, 8, cols), axis=0)
        xmo_ref[lev : lev + 1] = xm_ref[lev : lev + 1] + jnp.sum(mean, axis=0, keepdims=True)
        for half in range(cols // 256):
            lanes = slice(half * 256, (half + 1) * 256)
            inc = mm16(gt_ref[...], k_ref[:, lanes])
            xo_ref[lev, :, lanes] = (x_ref[lev, :, lanes].astype(F32) - inc).astype(BF16)


N_IN = 6


def first_kernel(*refs):
    ins, sites, outs, scratch = refs[:N_IN], refs[N_IN : N_IN + 4], refs[N_IN + 4 : N_IN + 7], refs[N_IN + 7 :]
    xo_ref, xmo_ref, share_ref = outs
    analyse(*ins, xo_ref, xmo_ref, *scratch)
    gather_sites(1, xo_ref, xmo_ref, *sites, share_ref)


def last_kernel(*refs):
    analyse(*refs)


def analysis_scratch(n, e, cols):
    nb = n // B

    def buf(*shape):
        return pltpu.VMEM(shape, F32)

    return [
        buf(n, e), pltpu.VMEM((n, e), BF16), buf(e, e), buf(nb + 1, e, e), buf(B, B), buf(B, B),
        buf(B, B), buf(B, e), buf(B, e), buf(8, e), buf(n + B, e), buf(nb + 1, 8, B), buf(nb, B),
        buf(nb, B, B), buf(nb, B), pltpu.VMEM((e, n), BF16), pltpu.VMEM((n, cols), BF16),
    ]


VMEM = pl.BlockSpec(memory_space=pltpu.VMEM)
PARAMS = pltpu.CompilerParams(vmem_limit_bytes=40 * 2**20)


def shards(
    perturb, mean_state, obs_value, obs_var, obs_weight, obs_tile, obs_col, obs_level,
    loc_horiz, loc_vert,
):
    levels, members, cols = perturb.shape
    batches, n = obs_tile.shape
    nb = n // B
    my_tile = lax.axis_index("horiz")
    first = lax.axis_index("lev") * levels
    near = lax.dynamic_slice_in_dim(loc_horiz, my_tile, 1, axis=1)
    damp = (near * lax.dynamic_slice_in_dim(loc_vert, first, levels, axis=1)).reshape(
        batches, levels, nb, B
    )
    sites = (obs_tile, obs_col, obs_level, obs_weight)
    values = obs_value.reshape(batches, nb, B)
    variances = obs_var.reshape(batches, nb, B)
    share_type = jax.ShapeDtypeStruct((2, 4, members // 8 + 1, 8, B), F32)
    state_types = (
        jax.ShapeDtypeStruct(perturb.shape, BF16),
        jax.ShapeDtypeStruct(mean_state.shape, F32),
    )
    scratch = analysis_scratch(n, members, cols)
    share = pl.pallas_call(
        gather_kernel, out_shape=share_type, in_specs=[VMEM] * 6, out_specs=VMEM,
        compiler_params=PARAMS, name="gather",
    )(perturb, mean_state, *sites)
    panel = sum_over_devices(share)
    perturb, mean_state, share = pl.pallas_call(
        first_kernel, out_shape=state_types + (share_type,), in_specs=[VMEM] * (N_IN + 4),
        out_specs=(VMEM,) * 3, scratch_shapes=scratch, compiler_params=PARAMS, name="analysis0",
    )(panel, perturb, mean_state, values[0], variances[0], damp[0], *sites)
    panel = sum_over_devices(share)
    return pl.pallas_call(
        last_kernel, out_shape=state_types, in_specs=[VMEM] * N_IN, out_specs=(VMEM,) * 2,
        scratch_shapes=scratch, compiler_params=PARAMS, name="analysis1",
    )(panel, perturb, mean_state, values[1], variances[1], damp[1])


def solution(mesh):
    return jax.shard_map(
        shards,
        mesh=mesh,
        in_specs=(P("lev", None, "horiz"), P("lev", "horiz")) + (P(),) * 8,
        out_specs=(P("lev", None, "horiz"), P("lev", "horiz")),
        check_vma=False,
    )
```

time: 1570 us -> 206 us (0.13)
  other arithmetic: 687 us -> 0.86 us
  waiting for transfers between devices: 319 us -> 0 us
  Pallas kernels: 0 us -> 196 us
  matrix products: 172 us -> 0 us
  local copies, waits for them, and re-layouts: 177 us -> 7.04 us
  blocking collectives: 153 us -> 0 us
  between operations: 27.1 us -> 0.72 us
  starting transfers between devices: 19.9 us -> 0 us
    another operation x71 -> x0, other arithmetic: 666 us -> none  [the longest x62 336 us: solve_batch(): factor = jnp.linalg.cholesky(innov_cov)]
    psum x2 -> x0, waiting for transfers between devices: 318 us -> none  [shards(): obs_rows, obs_means = lax.psum((site_rows, site_means), ('horiz', 'lev'))]
    pallas_call x0 -> x5, Pallas kernels: none -> 196 us  [the longest x2 84.6 us: sum_over_devices(): pl.pallas_call(sum_kernel, out_shape=jax.ShapeDtypeStruct(share.shape, F3...]
    psum x2 -> x0, blocking collectives: 153 us -> none  [shards(): obs_rows, obs_means = lax.psum((site_rows, site_means), ('horiz', 'lev'))]
    another operation x148 -> x0, matrix products: 146 us -> none  [the longest x28 52.6 us: solve_batch(): factor = jnp.linalg.cholesky(innov_cov)]
    another operation x231 -> x0, local copies, waits for them, and re-layouts: 106 us -> none  [the longest x93 47.3 us: solve_batch(): lax.linalg.triangular_solve(factor, left_solve, left_side=True, lower=Tru...]
    gather x8 -> x0, local copies, waits for them, and re-layouts: 40.9 us -> none  [the longest x2 12.3 us: pick_sites(): mean_cells[position + 1]]
    dot_general x14 -> x0, matrix products: 25.2 us -> none  [the longest x2 14.5 us: solve_batch(): jnp.dot(panel_rows, panel_rows.T, precision=lax.Precision.HIGHEST)]
  transfers between devices with their start and end apart: 6 -> 0, of which waited for: 4 -> 0; matrix products, arithmetic and copies ran while one was open for 3% -> 0% of each run, Pallas kernels for 0% -> 0%
where the time goes in v1:
time: 206 us; the launch traced here: 205 us
  Pallas kernels  196 us (95%)
  local copies, waits for them, and re-layouts  7.04 us (3%)
    pallas_call x2, Pallas kernels, sum_over_devices(): pl.pallas_call(sum_kernel, out_shape=jax.ShapeDtypeStruct(share.shape, F3...  84.6 us
    pallas_call x1, Pallas kernels, shards(): pl.pallas_call(first_kernel, out_shape=state_types + (share_type,), in_sp...  55.4 us
    pallas_call x1, Pallas kernels, shards(): pl.pallas_call(last_kernel, out_shape=state_types, in_specs=[VMEM] * N_IN...  54.4 us
    unnamed x16, local copies, waits for them, and re-layouts  5.46 us

profile of v1, /device:TPU:1, one launch (start us, length us, event | category | flops | bytes accessed | tf_op | source)
XLA Modules:
  0.0 205.0 jit_solution(17709211487658011736)
XLA Ops:
  0.6 0.0 copy-start
  0.6 0.9 copy-done
  1.6 0.9 dynamic-slice_multiply_fusion
  2.5 0.8 fusion.1
  3.3 0.8 fusion
  4.1 0.0 copy-start.1
  4.1 1.0 copy-done.1
  5.1 0.0 copy-start.2
  5.1 0.7 copy-done.2
  5.8 0.0 copy-start.3
  5.8 0.7 copy-done.3
  6.5 0.0 copy-start.4
  6.5 0.7 copy-done.4
  7.2 0.0 copy-start.5
  7.2 0.7 copy-done.5
  7.9 0.0 copy-start.6
  7.9 0.7 copy-done.6
  8.6 2.0 gather.1.c_ref
  10.6 46.1 %shard_map.113.refs_0_ = f32[2,4,33,8,128]{4,3,2,1,0:T(8,128)S(1)} custom-call(f32[2,4,33,8,128]{4,3,2,1,0:T(8,128)S(1)} %gather.1.c_ref), custom_call_target="tpu_custom_call" | custom-call | tf_op jit(solution)/shard_map/pallas_call | solution.py:192
  56.7 55.4 %analysis0.1 = (bf16[2,256,512]{2,1,0:T(8,128)(2,1)S(1)}, f32[2,512]{1,0:T(2,128)S(1)}, f32[2,4,33,8,128]{4,3,2,1,0:T(8,128)S(1)}) custom-call(f32[2,4,33,8,128]{4,3,2,1,0:T(8,128)S(1)} %shard_map.113.refs_0_, bf16[2,256,512]{2,1,0:T(8,128)(2,1)S(1)} %copy-done.1, f32[2,512]{1,0:T(2,128)S(1)} %copy-done.6, f32[8,128]{1,0:T(8,128)S(1)} %bitcast.19, ...), custom_call_target="tpu_custom_call" | custom-call | tf_op jit(solution)/shard_map/analysis0/pallas_call | solution.py:426
  112.1 38.4 %shard_map.114.refs_0_ = f32[2,4,33,8,128]{4,3,2,1,0:T(8,128)S(1)} custom-call(f32[2,4,33,8,128]{4,3,2,1,0:T(8,128)S(1)} %get-tuple-element.5.c_ref), custom_call_target="tpu_custom_call" | custom-call | tf_op jit(solution)/shard_map/pallas_call | solution.py:192
  150.6 54.4 %analysis1.1 = (bf16[2,256,512]{2,1,0:T(8,128)(2,1)}, f32[2,512]{1,0:T(2,128)}) custom-call(f32[2,4,33,8,128]{4,3,2,1,0:T(8,128)S(1)} %shard_map.114.refs_0_, bf16[2,256,512]{2,1,0:T(8,128)(2,1)S(1)} %get-tuple-element.6.refs_1_, f32[2,512]{1,0:T(2,128)S(1)} %get-tuple-element.7.refs_2_, f32[8,128]{1,0:T(8,128)S(1)} %bitcast.17, f32[8,128]{1,0:T(8,128)S(1)} %bitcast.18, ...), custom_call_target="tpu_custom_call" | custom-call | tf_op jit(solution)/shard_map/analysis1/pallas_call | solution.py:431
  (4 shorter events, 0.0 us)
Async XLA Ops:
  0.6 1.0 copy-start
  4.1 1.0 copy-start.1
  5.1 0.7 copy-start.2
  5.8 0.7 copy-start.3
  6.5 0.7 copy-start.4
  7.2 0.7 copy-start.5
  7.9 0.7 copy-start.6

commit v2 on v1

v2 whole, which is shorter than its diff:
```python
import functools
import jax
import jax.numpy as jnp
from jax import lax
from jax.experimental import pallas as pl
from jax.experimental.pallas import tpu as pltpu
from jax.sharding import PartitionSpec as P

F32 = jnp.float32
BF16 = jnp.bfloat16
HIGHEST = lax.Precision.HIGHEST
MESH = pl.DeviceIdType.MESH
B = 128
Q = 32
NT = ((1,), (1,))
TN = ((0,), (0,))
NN = ((1,), (0,))


def mm(a, b, dims=NN):
    return lax.dot_general(a, b, (dims, ((), ())), precision=HIGHEST, preferred_element_type=F32)


def mm16(a, b):
    return jnp.dot(a, b, preferred_element_type=F32)


def columns_of(rows):
    return jnp.concatenate([rows] * 16, axis=0).T


def rows_at(i):
    return pl.ds(pl.multiple_of(i * B, B), B)


def in_three(rows):
    hi = rows.astype(BF16).astype(F32)
    mid = (rows - hi).astype(BF16).astype(F32)
    low = rows - hi - mid
    at = lax.broadcasted_iota(jnp.int32, (16, rows.shape[1]), 0)
    return jnp.where(at == 0, hi, jnp.where(at == 1, mid, jnp.where(at == 2, low, 0.0))).astype(BF16)


def one_hot(rows, index):
    at = lax.broadcasted_iota(jnp.int32, (rows, index.shape[1]), 0)
    return jnp.where(at == index, 1.0, 0.0)


def after(tile, col, cols, tiles):
    wraps = col == cols - 1
    next_tile = jnp.where(wraps, jnp.where(tile == tiles - 1, 0, tile + 1), tile)
    return wraps, next_tile, jnp.where(wraps, 0, col + 1)


def gather_sites(batch, across, x_ref, xm_ref, sites, out_ref):
    tile_ref, col_ref, level_ref, frac_ref = sites
    levels, members, cols = x_ref.shape
    tiles = lax.axis_size("horiz")
    my_tile = lax.axis_index("horiz")
    first = lax.axis_index("lev") * levels
    row = lax.broadcasted_iota(jnp.int32, (8, B), 0)
    width = 2 * B
    means = [in_three(xm_ref[lev : lev + 1, :]) for lev in range(levels)]
    for jb in range(4):
        lanes = slice(jb * width, (jb + 1) * width)
        tile, col, level, frac = (
            ref[batch : batch + 1, lanes] for ref in (tile_ref, col_ref, level_ref, frac_ref)
        )
        wraps, next_tile, next_col = after(tile, col, cols, tiles)
        if not across:
            next_col = jnp.where(wraps, -1, next_col)
        vals = []
        for t, c in ((tile, col), (next_tile, next_col)):
            v = jnp.zeros((members, width), F32)
            m = jnp.zeros((16, width), F32)
            for lev in range(levels):
                pos = jnp.where((t == my_tile) & (level == first + lev), c, -1)
                hot = one_hot(cols, pos).astype(BF16)
                v = v + mm16(x_ref[lev], hot)
                m = m + mm16(means[lev], hot)
            vals.append((v, jnp.sum(m[0:8], axis=0, keepdims=True)))
        site = (1.0 - frac) * vals[0][0] + frac * vals[1][0]
        mean = (1.0 - frac) * vals[0][1] + frac * vals[1][1]
        for core in range(2):
            half = slice(core * B, (core + 1) * B)
            out_ref[core, jb, 0:32] = site[:, half].reshape(32, 8, B)
            out_ref[core, jb, 32] = jnp.where(row == 0, mean[:, half], 0.0)


class Place:
    def __init__(self):
        horiz = lax.axis_index("horiz")
        lev = lax.axis_index("lev")
        self.x, self.z = horiz // 8, horiz % 8
        self.y, self.core = lev // 2, lev % 2
        self.other = 1 - self.core
        self.xs = [self.x] + [(self.x + k) % 4 for k in range(1, 4)]
        self.ys = [self.y] + [(self.y + k) % 4 for k in range(1, 4)]
        self.ys_back = [self.y] + [(self.y - k + 4) % 4 for k in range(1, 4)]
        self.zs = [self.z] + [(self.z + k) % 8 for k in range(1, 8)]
        self.to_core = (horiz, self.y * 2 + self.other)
        self.to_y = [None] + [(horiz, self.ys[k] * 2 + self.core) for k in range(1, 4)]
        self.to_x = [None] + [(self.xs[k] * 8 + self.z, lev) for k in range(1, 4)]
        self.to_z = [None] + [(self.x * 8 + self.zs[k], lev) for k in range(1, 8)]
        self.peers = [self.to_core] + self.to_y[1:] + self.to_x[1:] + self.to_z[1:]
        self.home = 8 * self.x + self.z
        self.x8 = 8 * self.x
        self.xs8 = [8 * v for v in self.xs]
        self.cell_home = 33 + self.home
        self.cell_x8 = 33 + self.x8


def sum_phases(place, c_ref, o_ref, bufs, send, recv, cells):
    r0, a0, r1, a1, r2, a2, r3 = bufs
    core, other, x, y, z = place.core, place.other, place.x, place.y, place.z
    sem = iter(range(COPIES))

    def copy(src, dst, peer):
        k = next(sem)
        return lambda: pltpu.make_async_remote_copy(
            src_ref=src, dst_ref=dst, send_sem=send.at[k], recv_sem=recv.at[k],
            device_id=peer, device_id_type=MESH,
        )

    order = (1, 2, 3, 0)
    to_core = [
        copy(c_ref.at[other, place.ys[k]], r0.at[place.ys[k]], place.to_core) for k in order
    ]
    to_y = [copy(a0.at[place.ys[k]], r1.at[k - 1], place.to_y[k]) for k in range(1, 4)]
    to_x, to_z, back_z, back_x = [], [], [], []
    for k in range(1, 4):
        to_x.append(copy(a1.at[pl.ds(place.xs8[k], 8)], r2.at[k - 1, pl.ds(0, 8)], place.to_x[k]))
        to_x.append(copy(a1.at[pl.ds(32, 1)], r2.at[k - 1, pl.ds(8, 1)], place.to_x[k]))
    for k in range(1, 8):
        to_z.append(copy(a2.at[pl.ds(place.zs[k], 1)], r3.at[k - 1, pl.ds(0, 1)], place.to_z[k]))
        to_z.append(copy(a2.at[pl.ds(8, 1)], r3.at[k - 1, pl.ds(1, 1)], place.to_z[k]))
    starts = (place.home, place.cell_home) if cells else (place.home,)
    for k in range(1, 8):
        for s in starts:
            spot = o_ref.at[core, y, pl.ds(s, 1)]
            back_z.append(copy(spot, spot, place.to_z[k]))
    starts = (place.x8, place.cell_x8) if cells else (place.x8,)
    for k in range(1, 4):
        for s in starts:
            spot = o_ref.at[core, y, pl.ds(s, 8)]
            back_x.append(copy(spot, spot, place.to_x[k]))
    spot = o_ref.at[core, y]
    back_y = [copy(spot, spot, place.to_y[k]) for k in range(1, 4)]
    back_core = []
    for k in range(4):
        spot = o_ref.at[core, place.ys_back[k]]
        back_core.append(copy(spot, spot, place.to_core))

    def start(copies):
        for c in copies:
            c().start()

    def arrive(copies):
        for c in copies:
            c().wait_recv()

    def begin():
        start(to_core)

    def add_core():
        for k, c in zip(order, to_core):
            c().wait_recv()
            yk = place.ys[k]
            a0[yk] = c_ref[core, yk] + r0[yk]
            if k:
                to_y[k - 1]().start()

    def add_y():
        arrive(to_y)
        a1[...] = (a0[y] + r1[0]) + (r1[1] + r1[2])
        start(to_x)

    def add_x():
        arrive(to_x)
        a2[0:8] = (a1[pl.ds(place.x8, 8)] + r2[0, 0:8]) + (r2[1, 0:8] + r2[2, 0:8])
        a2[8:9] = (a1[32:33] + r2[0, 8:9]) + (r2[1, 8:9] + r2[2, 8:9])
        start(to_z)

    def add_z():
        arrive(to_z)
        mine = a2[z]
        mean = a2[8]
        for k in range(7):
            mine = mine + r3[k, 0]
            mean = mean + r3[k, 1]
        o_ref[core, y, place.home] = mine
        o_ref[core, y, 32] = mean
        start(back_z)

    def return_x():
        arrive(back_z)
        start(back_x)

    def return_y():
        arrive(back_x)
        start(back_y)
        start(back_core[:1])

    def return_core():
        for k in range(3):
            back_y[k]().wait_recv()
            back_core[k + 1]().start()

    def end():
        arrive(back_core)
        for group in (to_core, to_y, to_x, to_z, back_z, back_x, back_y, back_core):
            for c in group:
                c().wait_send()

    return [begin, add_core, add_y, add_x, add_z, return_x, return_y, return_core, end]


COPIES = 4 + 3 + 6 + 14 + 14 + 6 + 3 + 4


def sum_buffers():
    def buf(*shape):
        return pltpu.VMEM(shape + (8, B), F32)

    return [buf(4, 33), buf(4, 33), buf(3, 33), buf(33), buf(3, 9), buf(9), buf(7, 2)]


def factor_block(s, dcol):
    nt = Q // 8
    row = lax.broadcasted_iota(jnp.int32, (8, B), 0)
    eye = jnp.where(
        lax.broadcasted_iota(jnp.int32, (B, B), 0) == lax.broadcasted_iota(jnp.int32, (B, B), 1),
        1.0,
        0.0,
    )
    m, a, z = s, eye, eye
    out_a, out_z = [], []
    for o in range(0, B, Q):
        w_t = [m[8 * t : 8 * t + 8] for t in range(nt)]
        a_t = [a[8 * t : 8 * t + 8] for t in range(nt)]
        z_t = [z[8 * t : 8 * t + 8] for t in range(nt)]
        cols = [
            [
                None if t < c // 8 else jnp.broadcast_to(w_t[t][:, o + c : o + c + 1], (8, B))
                for t in range(nt)
            ]
            for c in range(Q)
        ]
        for r in range(Q):
            tr, rr = r // 8, r % 8
            p = cols[r][tr][rr : rr + 1]
            rs = lax.rsqrt(p)
            l = [None if t < tr else cols[r][t] * rs for t in range(nt)]
            u = w_t[tr][rr : rr + 1] * rs
            av = a_t[tr][rr : rr + 1] * rs
            zv = z_t[tr][rr : rr + 1] / (p * rs + dcol[o + r : o + r + 1])
            for c in range(r + 1, Q):
                f = l[c // 8][c % 8 : c % 8 + 1]
                for t in range(c // 8, nt):
                    cols[c][t] = cols[c][t] - l[t] * f
            for t in range(tr, nt):
                lt = l[t] if t > tr else jnp.where(row > rr, l[t], 0.0)
                for rows, v in ((w_t, u), (a_t, av), (z_t, zv)):
                    new = rows[t] - lt * v
                    if t == tr:
                        new = jnp.where(row == rr, jnp.broadcast_to(v, (8, B)), new)
                    rows[t] = new
        u_b, a_b, z_b = (jnp.concatenate(rows, 0) for rows in (w_t, a_t, z_t))
        out_a.append(a_b)
        out_z.append(z_b)
        if o + Q < B:
            step = mm(u_b, jnp.concatenate([u_b, a_b, z_b], 1), TN)[o + Q :]
            m = m[Q:] - step[:, :B]
            a = a[Q:] - step[:, B : 2 * B]
            z = z[Q:] - step[:, 2 * B :]
    return jnp.concatenate(out_a, 0), jnp.concatenate(out_z, 0)


def rows8(ref, row):
    line = ref[row, :]
    return jnp.concatenate([line[:, k : k + B] for k in range(0, line.shape[1], B)], axis=0)


def analyse(site_of, mean_of, values, variances, damping, x_ref, xm_ref, hooks, between, scratch):
    (a_ref, yb_ref, p_ref, qs_ref, s_ref, linv_ref, minv_ref, t1_ref, aq_ref, qv_ref, lz_ref,
     d_ref, var_ref, vcol_ref, gt_ref, k_ref) = scratch
    levels, members, cols = x_ref.shape
    n = a_ref.shape[0]
    nb = n // B
    c = 1.0 / (members - 1.0) ** 0.5

    def square(k):
        return lax.broadcasted_iota(jnp.int32, (k, k), 0) == lax.broadcasted_iota(
            jnp.int32, (k, k), 1
        )

    eye_m = jnp.where(square(members), 1.0, 0.0)
    diag = square(B)
    for i in range(nb):
        y_i = site_of(i).T
        a_ref[i * B : (i + 1) * B] = y_i * c
        yb_ref[i * B : (i + 1) * B] = y_i.astype(BF16)
        d_ref[i : i + 1] = values[i : i + 1] - mean_of(i)
    var_ref[...] = variances
    var_cols = columns_of(variances)
    for i in range(nb):
        vcol_ref[i] = jnp.broadcast_to(var_cols[:, i : i + 1], (B, B))
    p_ref[...] = eye_m
    qs_ref[0] = eye_m * (1.0 / c)
    a_0 = a_ref[0:B]
    s_ref[...] = mm(a_0, a_0, NT) + jnp.where(diag, var_ref[0:1], 0.0)
    for ref in (linv_ref, minv_ref, t1_ref, aq_ref, qv_ref):
        ref[...] = jnp.zeros_like(ref)

    def finish_previous(i):
        linv, minv, t1 = linv_ref[...], minv_ref[...], t1_ref[...]
        ip = jnp.maximum(i - 1, 0)
        v = mm(linv, t1)
        z = mm(minv, aq_ref[...])
        lz_ref[rows_at(i)] = mm(linv, z, TN)
        p = p_ref[...] - mm(v, v, TN)
        q = qs_ref[ip] - mm(v, z, TN)
        qv = qv_ref[...]
        rhs = d_ref[pl.ds(ip, 1)] - mm(qv, a_ref[rows_at(ip)], NT)
        qv = qv + mm(mm(rhs, linv, NT), v)
        return p, q, qv

    def step(i, carry):
        p, q, qv = finish_previous(i)
        i_next = jnp.minimum(i + 1, nb - 1)
        a_i = a_ref[rows_at(i)]
        a_n = a_ref[rows_at(i_next)]
        t1 = mm(a_i, p)
        t1_n = mm(a_n, p)
        s_nn = mm(t1_n, a_n, NT) + jnp.where(diag, var_ref[pl.ds(i_next, 1)], 0.0)
        s_ni = mm(t1_n, a_i, NT)
        aq = mm(a_i, q)
        linv, minv = factor_block(s_ref[...], jnp.sqrt(vcol_ref[i]))
        l_ni = mm(s_ni, linv, NT)
        s_ref[...] = s_nn - mm(l_ni, l_ni, NT)
        linv_ref[...] = linv
        minv_ref[...] = minv
        t1_ref[...] = t1
        aq_ref[...] = aq
        p_ref[...] = p
        qs_ref[i] = q
        qv_ref[...] = qv
        for k, hook in enumerate(hooks):
            pl.when(i == k)(hook)
        return carry

    lax.fori_loop(0, nb, step, 0)
    p, q, qv = finish_previous(nb)

    def over_obs(rows):
        total = jnp.zeros((8, members), F32)
        for i in range(nb):
            total = total + mm(jnp.broadcast_to(rows[i : i + 1], (8, B)), a_ref[i * B : (i + 1) * B])
        return total

    def times_a(v):
        return jnp.concatenate(
            [mm(v, a_ref[i * B : (i + 1) * B], NT)[0:1] for i in range(nb)], axis=0
        )

    d, var = d_ref[...], var_ref[...]
    w = (d - times_a(qv)) / var
    rest = d - var * w - times_a(over_obs(w))
    w = w + (rest - times_a(mm(over_obs(rest / var), p))) / var
    w_cols = columns_of(w)

    for i in range(nb):
        g = lz_ref[(i + 1) * B : (i + 2) * B]
        if i < nb - 1:
            inv = 1.0 / vcol_ref[i]
            g = g - mm(a_ref[i * B : (i + 1) * B], qs_ref[i + 1] - q) * jnp.concatenate([inv, inv], 1)
        gt_ref[:, i * B : (i + 1) * B] = g.T.astype(BF16)

    w_lines = [w_cols[:, i : i + 1] for i in range(nb)]
    between(w_lines)
    for lev in range(levels):
        damp_cols = columns_of(damping[lev] * (1.0 / (members - 1.0)))
        slab = x_ref[lev]
        inc, mean = increments(
            lambda i: mm16(yb_ref[i * B : (i + 1) * B], slab) * damp_cols[:, i : i + 1],
            w_lines, gt_ref, k_ref,
        )
        xm_ref[lev : lev + 1] = xm_ref[lev : lev + 1] + mean
        x_ref[lev] = (slab.astype(F32) - inc).astype(BF16)


def increments(gain_of, w_lines, gt_ref, k_ref):
    mean = 0.0
    for i, w in enumerate(w_lines):
        f = gain_of(i)
        k_ref[i * B : (i + 1) * B] = f.astype(BF16)
        mean = mean + jnp.sum((f * w).reshape(B // 8, 8, f.shape[1]), axis=0)
    inc = [mm16(gt_ref[...], k_ref[:, c : c + 256]) for c in range(0, k_ref.shape[1], 256)]
    return jnp.concatenate(inc, axis=1), jnp.sum(mean, axis=0, keepdims=True)


def stack_three(rows):
    hi = rows.astype(BF16)
    mid = (rows - hi.astype(F32)).astype(BF16)
    low = (rows - hi.astype(F32) - mid.astype(F32)).astype(BF16)
    return jnp.concatenate([hi, mid, low], axis=0)


def pick_t(table, hot):
    return lax.dot_general(table, hot, (TN, ((), ())), preferred_element_type=F32)


def update_sites(share_ref, lh_ref, lv_ref, sites, scratch, w_lines, yt_ref, ym_ref, cells_ref):
    tile_ref, col_ref, level_ref, frac_ref = sites
    yb_ref, gt_ref, k_ref = scratch[1], scratch[14], scratch[15]
    n, members = yb_ref.shape
    cols = k_ref.shape[1]
    tiles, levels = lh_ref.shape[1], lv_ref.shape[1]
    lh = stack_three(lh_ref[0] * (1.0 / (members - 1.0)))
    lv = stack_three(lv_ref[0])

    def updated(slab, mean, tile, level):
        hi = slab.astype(BF16)
        low = (slab - hi.astype(F32)).astype(BF16)
        hot_t = one_hot(tiles, tile).astype(BF16)
        hot_l = one_hot(levels, level).astype(BF16)
        hot_t = jnp.concatenate([hot_t] * 3, axis=0)
        hot_l = jnp.concatenate([hot_l] * 3, axis=0)

        def gain_of(i):
            y_i = yb_ref[i * B : (i + 1) * B]
            damp = pick_t(lh[:, i * B : (i + 1) * B], hot_t) * pick_t(lv[:, i * B : (i + 1) * B], hot_l)
            return (mm16(y_i, hi) + mm16(y_i, low)) * damp

        inc, gained = increments(gain_of, w_lines, gt_ref, k_ref)
        return slab - inc, mean + gained

    at = lax.broadcasted_iota(jnp.int32, (8 * tiles, B), 0)
    cell = lax.broadcasted_iota(jnp.int32, (8 * tiles, B), 1)
    t_at, r_at = at // 8, at % 8
    top, bottom, middle = [], [], []
    for pair in range(4):
        parts = [0.0, 0.0, 0.0]
        for core in range(2):
            group = share_ref[core, pair, 33 : 33 + tiles].reshape(8 * tiles, B)
            c = cell - core * 2 * tiles
            lev_at = c // tiles
            hit = (c >= 0) & (c < 2 * tiles) & (c % tiles == t_at)
            for half in range(2):
                sel = jnp.where(hit & (r_at == 2 * lev_at + half), 1.0, 0.0).astype(BF16)
                parts[half] = parts[half] + pick_t(group.astype(BF16), sel)
            sel = jnp.where(hit & (r_at == 4 + lev_at), 1.0, 0.0)
            parts[2] = parts[2] + mm(group, sel, TN)[0:1]
        top.append(parts[0])
        bottom.append(parts[1])
        middle.append(parts[2])
    cells = jnp.concatenate([jnp.concatenate(top, 1), jnp.concatenate(bottom, 1)], 0)
    cell_mean = jnp.concatenate(middle, 1)
    index = lax.broadcasted_iota(jnp.int32, (1, cols), 1)
    cells, cell_mean = updated(cells, cell_mean, index % tiles, index // tiles)
    cells_ref[...] = cells.astype(BF16)
    cell_mean = in_three(cell_mean)
    for half in range(n // cols):
        lanes = slice(half * cols, (half + 1) * cols)
        tile, col, level, frac = (
            ref[1:2, lanes] for ref in (tile_ref, col_ref, level_ref, frac_ref)
        )
        spots = [(p % 2, p // 2) for p in range(4 * half, 4 * half + 4)]
        slab = jnp.concatenate([share_ref[c, y, 0:32].reshape(members, B) for c, y in spots], 1)
        mean = jnp.concatenate([share_ref[c, y, 32][0:1] for c, y in spots], 1)
        slab, mean = updated(slab, mean, tile, level)
        wraps, next_tile, _ = after(tile, col, cols, tiles)
        hot = one_hot(cols, jnp.where(wraps, level * tiles + next_tile, -1)).astype(BF16)
        yt_ref[:, lanes] = slab + frac * mm16(cells_ref[...], hot)
        ym_ref[0:1, lanes] = mean + frac * jnp.sum(mm16(cell_mean, hot)[0:8], axis=0, keepdims=True)


def whole_kernel(*refs):
    args, (x_ref, xm_ref), refs = refs[:10], refs[10:12], refs[12:]
    held, refs = refs[:8], refs[8:]
    share0, panel0, share1, panel1, refs = refs[0], refs[1], refs[2], refs[3], refs[4:]
    bufs0, bufs1, refs = refs[:7], refs[7:14], refs[14:]
    (load, send0, recv0, send1, recv1), refs = refs[:5], refs[5:]
    (yt_ref, ym_ref, cells_ref), scratch = refs[:3], refs[3:]

    barrier = pltpu.get_barrier_semaphore()
    place = Place()
    for peer in place.peers:
        pl.semaphore_signal(barrier, inc=1, device_id=peer, device_id_type=MESH)
    copies = [
        pltpu.make_async_copy(src, dst, load.at[k])
        for k, (src, dst) in enumerate(zip(args, (x_ref, xm_ref) + tuple(held)))
    ]
    for copy in copies:
        copy.start()
    for copy in copies:
        copy.wait()
    val_ref, var_ref, frac_ref, tile_ref, col_ref, level_ref, lh_ref, lv_ref = held
    sites = (tile_ref, col_ref, level_ref, frac_ref)
    levels, members, cols = x_ref.shape

    gather_sites(0, True, x_ref, xm_ref, sites, share0)
    pl.semaphore_wait(barrier, len(place.peers))
    first_sum = sum_phases(place, share0, panel0, bufs0, send0, recv0, False)
    second_sum = sum_phases(place, share1, panel1, bufs1, send1, recv1, True)
    first_sum[0]()
    gather_sites(1, False, x_ref, xm_ref, sites, share1)
    r16 = lax.broadcasted_iota(jnp.int32, (B, B), 0)
    own = jnp.zeros((8, B), F32)
    row = lax.broadcasted_iota(jnp.int32, (8, B), 0)
    for lev in range(levels):
        for half in range(2):
            block = x_ref[lev, half * B : (half + 1) * B, 0:B].astype(F32).T
            own = jnp.where(row == 2 * lev + half, block[0:1], own)
        own = jnp.where(row == 4 + lev, xm_ref[lev : lev + 1, 0:1], own)
    panel1[place.core, place.y, place.cell_home] = own
    for phase in first_sum[1:]:
        phase()
    second_sum[0]()

    def damping(batch):
        near = rows8(lh_ref.at[batch], pl.ds(place.home, 1))
        first = lax.axis_index("lev") * levels
        return [near * rows8(lv_ref.at[batch], pl.ds(first + lev, 1)) for lev in range(levels)]

    def between(w_lines):
        second_sum[8]()
        update_sites(panel1, lh_ref, lv_ref, sites, scratch, w_lines, yt_ref, ym_ref, cells_ref)

    hooks = second_sum[1:7] + [lambda: None, second_sum[7]]
    analyse(
        lambda i: panel0[i % 2, i // 2, 0:32].reshape(members, B),
        lambda i: panel0[i % 2, i // 2, 32][0:1],
        rows8(val_ref, slice(0, 1)), rows8(var_ref, slice(0, 1)), damping(0), x_ref, xm_ref,
        hooks, between, scratch,
    )
    analyse(
        lambda i: yt_ref[:, i * B : (i + 1) * B],
        lambda i: ym_ref[0:1, i * B : (i + 1) * B],
        rows8(val_ref, slice(1, 2)), rows8(var_ref, slice(1, 2)), damping(1), x_ref, xm_ref,
        [], lambda w_lines: None, scratch,
    )


def analysis_scratch(n, e, cols):
    nb = n // B

    def buf(*shape):
        return pltpu.VMEM(shape, F32)

    return [
        buf(n, e), pltpu.VMEM((n, e), BF16), buf(e, e), buf(nb + 1, e, e), buf(B, B), buf(B, B),
        buf(B, B), buf(B, e), buf(B, e), buf(8, e), buf(n + B, e), buf(nb, B), buf(nb, B),
        buf(nb, B, B), pltpu.VMEM((e, n), BF16), pltpu.VMEM((n, cols), BF16),
    ]


def shards(*args):
    perturb, mean_state, obs_value = args[:3]
    levels, members, cols = perturb.shape
    n = obs_value.shape[1]
    vm = pl.BlockSpec(memory_space=pltpu.VMEM)
    share = pltpu.VMEM((2, 4, members // 8 + 1, 8, B), F32)
    dma = pltpu.SemaphoreType.DMA
    return pl.pallas_call(
        whole_kernel,
        out_shape=(
            jax.ShapeDtypeStruct(perturb.shape, BF16),
            jax.ShapeDtypeStruct(mean_state.shape, F32),
        ),
        in_specs=[pl.BlockSpec(memory_space=pl.ANY)] * len(args),
        out_specs=(vm, vm),
        scratch_shapes=[pltpu.VMEM(a.shape, a.dtype) for a in args[2:]]
        + [share, share, share, pltpu.VMEM((2, 4, members // 8 + 33, 8, B), F32)]
        + sum_buffers()
        + sum_buffers()
        + [dma((len(args),))] + [dma((COPIES,))] * 4
        + [pltpu.VMEM((members, n), F32), pltpu.VMEM((8, n), F32), pltpu.VMEM((members, cols), BF16)]
        + analysis_scratch(n, members, cols),
        compiler_params=pltpu.CompilerParams(
            collective_id=0, has_side_effects=True, vmem_limit_bytes=48 * 2**20
        ),
        name="analysis",
    )(*args)


def solution(mesh):
    return jax.shard_map(
        shards,
        mesh=mesh,
        in_specs=(P("lev", None, "horiz"), P("lev", "horiz")) + (P(),) * 8,
        out_specs=(P("lev", None, "horiz"), P("lev", "horiz")),
        check_vma=False,
    )
```

time: 206 us -> 177 us (0.86)
  Pallas kernels: 196 us -> 166 us
  local copies, waits for them, and re-layouts: 7.04 us -> 9.14 us
    pallas_call x5 -> x1, Pallas kernels: 196 us -> 166 us  [shards(): pl.pallas_call(whole_kernel, out_shape=(jax.ShapeDtypeStruct(perturb.shap...]
    unnamed x16 -> x22, local copies, waits for them, and re-layouts: 5.46 us -> 9.14 us
where the time goes in v2:
time: 177 us; the launch traced here: 176 us
  Pallas kernels  166 us (94%)
  local copies, waits for them, and re-layouts  9.14 us (5%)
    pallas_call x1, Pallas kernels, shards(): pl.pallas_call(whole_kernel, out_shape=(jax.ShapeDtypeStruct(perturb.shap...  166 us
    unnamed x22, local copies, waits for them, and re-layouts  9.14 us

profile of v2, /device:TPU:1, one launch (start us, length us, event | category | flops | bytes accessed | tf_op | source)
XLA Modules:
  0.0 176.1 jit_solution(2242957577812250731)
XLA Ops:
  0.6 0.0 copy-start
  0.6 1.0 copy-done
  1.7 0.0 copy-start.1
  1.7 0.9 copy-done.1
  2.6 0.0 copy-start.2
  2.6 0.9 copy-done.2
  3.5 0.0 copy-start.3
  3.5 0.7 copy-done.3
  4.2 0.0 copy-start.4
  4.2 0.7 copy-done.4
  4.9 0.0 copy-start.5
  4.9 0.7 copy-done.5
  5.6 0.0 copy-start.6
  5.6 0.7 copy-done.6
  6.3 0.0 copy-start.7
  6.3 0.7 copy-done.7
  7.0 0.0 copy-start.8
  7.0 0.7 copy-done.8
  7.7 0.0 copy-start.9
  7.7 0.7 copy-done.9
  8.4 166.3 %analysis.1 = (bf16[2,256,512]{2,1,0:T(8,128)(2,1)S(1)}, f32[2,512]{1,0:T(2,128)S(1)}) custom-call(bf16[2,256,512]{2,1,0:T(8,128)(2,1)S(1)} %copy-done, f32[2,512]{1,0:T(2,128)S(1)} %copy-done.9, f32[2,1024]{1,0:T(2,128)S(1)} %copy-done.3, f32[2,1024]{1,0:T(2,128)S(1)} %copy-done.4, f32[2,1024]{1,0:T(2,128)S(1)} %copy-done.5, s32[2,1024]{1,0:T(2,128)S(1)} %copy-done.6, ...), custom_call_target="tpu_custom_call" | custom-call | tf_op jit(solution)/shard_map/analysis/pallas_call | solution.py:565
  174.7 0.8 copy.14
  175.5 0.6 copy.15
Async XLA Ops:
  0.6 1.0 copy-start
  1.7 0.9 copy-start.1
  2.6 0.9 copy-start.2
  3.5 0.7 copy-start.3
  4.2 0.7 copy-start.4
  4.9 0.7 copy-start.5
  5.6 0.7 copy-start.6
  6.3 0.7 copy-start.7
  7.0 0.7 copy-start.8
  7.7 0.7 copy-start.9

commit v3 on v2

--- a/solution.py
+++ b/solution.py
@@ -11,7 +11,8 @@
 HIGHEST = lax.Precision.HIGHEST
 MESH = pl.DeviceIdType.MESH
 B = 128
-Q = 32
+SUB = 16
+Q = 64
 NT = ((1,), (1,))
 TN = ((0,), (0,))
 NN = ((1,), (0,))
@@ -228,51 +229,61 @@
 def factor_block(s, dcol):
     nt = Q // 8
     row = lax.broadcasted_iota(jnp.int32, (8, B), 0)
+    lane = lax.broadcasted_iota(jnp.int32, (8, B), 1)
     eye = jnp.where(
         lax.broadcasted_iota(jnp.int32, (B, B), 0) == lax.broadcasted_iota(jnp.int32, (B, B), 1),
         1.0,
         0.0,
     )
-    m, a, z = s, eye, eye
+    both, shifted = s, eye
     out_a, out_z = [], []
     for o in range(0, B, Q):
-        w_t = [m[8 * t : 8 * t + 8] for t in range(nt)]
-        a_t = [a[8 * t : 8 * t + 8] for t in range(nt)]
-        z_t = [z[8 * t : 8 * t + 8] for t in range(nt)]
-        cols = [
-            [
-                None if t < c // 8 else jnp.broadcast_to(w_t[t][:, o + c : o + c + 1], (8, B))
-                for t in range(nt)
-            ]
-            for c in range(Q)
-        ]
-        for r in range(Q):
-            tr, rr = r // 8, r % 8
-            p = cols[r][tr][rr : rr + 1]
-            rs = lax.rsqrt(p)
-            l = [None if t < tr else cols[r][t] * rs for t in range(nt)]
-            u = w_t[tr][rr : rr + 1] * rs
-            av = a_t[tr][rr : rr + 1] * rs
-            zv = z_t[tr][rr : rr + 1] / (p * rs + dcol[o + r : o + r + 1])
-            for c in range(r + 1, Q):
-                f = l[c // 8][c % 8 : c % 8 + 1]
-                for t in range(c // 8, nt):
-                    cols[c][t] = cols[c][t] - l[t] * f
-            for t in range(tr, nt):
-                lt = l[t] if t > tr else jnp.where(row > rr, l[t], 0.0)
-                for rows, v in ((w_t, u), (a_t, av), (z_t, zv)):
-                    new = rows[t] - lt * v
-                    if t == tr:
-                        new = jnp.where(row == rr, jnp.broadcast_to(v, (8, B)), new)
-                    rows[t] = new
-        u_b, a_b, z_b = (jnp.concatenate(rows, 0) for rows in (w_t, a_t, z_t))
-        out_a.append(a_b)
+        w_t = [both[8 * t : 8 * t + 8] for t in range(nt)]
+        z_t = [shifted[8 * t : 8 * t + 8] for t in range(nt)]
+        for sub in range(0, Q, SUB):
+            begin, end = o + sub, o + sub + SUB
+            own = (lane >= begin) & (lane < end)
+            cols = {}
+            for c in range(sub, sub + SUB):
+                cols[c] = [
+                    None if t < c // 8 else jnp.broadcast_to(w_t[t][:, o + c : o + c + 1], (8, B))
+                    for t in range(nt)
+                ]
+            for t in range(sub // 8, nt):
+                unit = lane == row + (o + 8 * t)
+                if t < (sub + SUB) // 8:
+                    w_t[t] = jnp.where(own, jnp.where(unit, 1.0, 0.0), w_t[t])
+                else:
+                    w_t[t] = jnp.where(own, 0.0, w_t[t])
+            for r in range(sub, sub + SUB):
+                tr, rr = r // 8, r % 8
+                p = cols[r][tr][rr : rr + 1]
+                rs = lax.rsqrt(p)
+                l = [None if t < tr else cols[r][t] * rs for t in range(nt)]
+                for c in range(r + 1, sub + SUB):
+                    f = l[c // 8][c % 8 : c % 8 + 1]
+                    for t in range(c // 8, nt):
+                        cols[c][t] = cols[c][t] - l[t] * f
+                scale = 1.0 / (p * rs + dcol[o + r : o + r + 1])
+                for rows, v in ((w_t, w_t[tr][rr : rr + 1] * rs), (z_t, z_t[tr][rr : rr + 1] * scale)):
+                    for t in range(tr, nt):
+                        lt = l[t] if t > tr else jnp.where(row > rr, l[t], 0.0)
+                        new = rows[t] - lt * v
+                        if t == tr:
+                            new = jnp.where(row == rr, jnp.broadcast_to(v, (8, B)), new)
+                        rows[t] = new
+            if sub + SUB < Q:
+                ahead = (lane >= end) & (lane < o + Q)
+                for t in range(sub // 8, (sub + SUB) // 8):
+                    w_t[t] = jnp.where(ahead, 0.0, w_t[t])
+        u_b, z_b = jnp.concatenate(w_t, 0), jnp.concatenate(z_t, 0)
+        out_a.append(jnp.where(lax.broadcasted_iota(jnp.int32, (Q, B), 1) < o + Q, u_b, 0.0))
         out_z.append(z_b)
         if o + Q < B:
-            step = mm(u_b, jnp.concatenate([u_b, a_b, z_b], 1), TN)[o + Q :]
-            m = m[Q:] - step[:, :B]
-            a = a[Q:] - step[:, B : 2 * B]
-            z = z[Q:] - step[:, 2 * B :]
+            step = mm(u_b, jnp.concatenate([u_b, z_b], 1), TN)[o + Q :]
+            at = lax.broadcasted_iota(jnp.int32, (B - o - Q, B), 1)
+            both = jnp.where((at >= o) & (at < o + Q), 0.0, both[Q:]) - step[:, :B]
+            shifted = shifted[Q:] - step[:, B:]
     return jnp.concatenate(out_a, 0), jnp.concatenate(out_z, 0)
 
 
@@ -333,11 +344,11 @@
         t1 = mm(a_i, p)
         t1_n = mm(a_n, p)
         s_nn = mm(t1_n, a_n, NT) + jnp.where(diag, var_ref[pl.ds(i_next, 1)], 0.0)
-        s_ni = mm(t1_n, a_i, NT)
+        s_in = mm(a_i, t1_n, NT)
         aq = mm(a_i, q)
         linv, minv = factor_block(s_ref[...], jnp.sqrt(vcol_ref[i]))
-        l_ni = mm(s_ni, linv, NT)
-        s_ref[...] = s_nn - mm(l_ni, l_ni, NT)
+        l_in = mm(linv, s_in)
+        s_ref[...] = s_nn - mm(l_in, l_in, TN)
         linv_ref[...] = linv
         minv_ref[...] = minv
         t1_ref[...] = t1
@@ -568,7 +579,7 @@
             jax.ShapeDtypeStruct(perturb.shape, BF16),
             jax.ShapeDtypeStruct(mean_state.shape, F32),
         ),
-        in_specs=[pl.BlockSpec(memory_space=pl.ANY)] * len(args),
+        in_specs=[pl.BlockSpec(memory_space=pltpu.HBM)] * len(args),
         out_specs=(vm, vm),
         scratch_shapes=[pltpu.VMEM(a.shape, a.dtype) for a in args[2:]]
         + [share, share, share, pltpu.VMEM((2, 4, members // 8 + 33, 8, B), F32)]
@@ -578,7 +589,7 @@
         + [pltpu.VMEM((members, n), F32), pltpu.VMEM((8, n), F32), pltpu.VMEM((members, cols), BF16)]
         + analysis_scratch(n, members, cols),
         compiler_params=pltpu.CompilerParams(
-            collective_id=0, has_side_effects=True, vmem_limit_bytes=48 * 2**20
+            collective_id=0, has_side_effects=True, vmem_limit_bytes=60 * 2**20
         ),
         name="analysis",
     )(*args)

time: 177 us -> 155 us (0.88)
  Pallas kernels: 166 us -> 150 us
  local copies, waits for them, and re-layouts: 9.14 us -> 2.47 us
    pallas_call x1, Pallas kernels: 166 us -> 150 us  [shards(): pl.pallas_call(whole_kernel, out_shape=(jax.ShapeDtypeStruct(perturb.shap...]
    unnamed x22 -> x4, local copies, waits for them, and re-layouts: 9.14 us -> 2.47 us
where the time goes in v3:
time: 155 us; the launch traced here: 154 us
  Pallas kernels  150 us (97%)
  local copies, waits for them, and re-layouts  2.47 us (2%)
    pallas_call x1, Pallas kernels, shards(): pl.pallas_call(whole_kernel, out_shape=(jax.ShapeDtypeStruct(perturb.shap...  150 us

profile of v3, /device:TPU:1, one launch (start us, length us, event | category | flops | bytes accessed | tf_op | source)
XLA Modules:
  0.0 153.6 jit_solution(15030113439383653189)
XLA Ops:
  0.6 150.5 %analysis.1 = (bf16[2,256,512]{2,1,0:T(8,128)(2,1)}, f32[2,512]{1,0:T(2,128)}) custom-call(bf16[2,256,512]{2,1,0:T(8,128)(2,1)} %refs_0_.1, f32[2,512]{1,0:T(2,128)} %refs_1_.1, f32[2,1024]{1,0:T(2,128)} %refs_2_.1, f32[2,1024]{1,0:T(2,128)} %refs_3_.1, f32[2,1024]{1,0:T(2,128)} %refs_4_.1, s32[2,1024]{1,0:T(2,128)} %refs_5_.1, s32[2,1024]{1,0:T(2,128)} %refs_6_.1, ...), custom_call_target="tpu_custom_call" | custom-call | tf_op jit(solution)/shard_map/analysis/pallas_call | solution.py:576
  151.1 0.0 copy-start
  151.1 1.9 %copy.14 = bf16[2,256,512]{2,1,0:T(8,128)(2,1)} copy(bf16[2,256,512]{2,1,0:T(8,128)(2,1)} %get-tuple-element.4) | data formatting | bytes 1048576
  153.0 0.0 copy-done
  153.0 0.6 copy.15
Async XLA Ops:
  151.1 1.9 %copy-start = (f32[2,512]{1,0:T(2,128)S(1)}, f32[2,512]{1,0:T(2,128)}, u32[]{:S(2)}) copy-start(f32[2,512]{1,0:T(2,128)} %get-tuple-element.5) | copy-start | bytes 12292

commit v4 on v3

--- a/solution.py
+++ b/solution.py
@@ -53,7 +53,7 @@
     return wraps, next_tile, jnp.where(wraps, 0, col + 1)
 
 
-def gather_sites(batch, across, x_ref, xm_ref, sites, out_ref):
+def gather_sites(batch, across, quarters, x_ref, xm_ref, sites, put):
     tile_ref, col_ref, level_ref, frac_ref = sites
     levels, members, cols = x_ref.shape
     tiles = lax.axis_size("horiz")
@@ -62,7 +62,7 @@
     row = lax.broadcasted_iota(jnp.int32, (8, B), 0)
     width = 2 * B
     means = [in_three(xm_ref[lev : lev + 1, :]) for lev in range(levels)]
-    for jb in range(4):
+    for jb in quarters:
         lanes = slice(jb * width, (jb + 1) * width)
         tile, col, level, frac = (
             ref[batch : batch + 1, lanes] for ref in (tile_ref, col_ref, level_ref, frac_ref)
@@ -84,8 +84,7 @@
         mean = (1.0 - frac) * vals[0][1] + frac * vals[1][1]
         for core in range(2):
             half = slice(core * B, (core + 1) * B)
-            out_ref[core, jb, 0:32] = site[:, half].reshape(32, 8, B)
-            out_ref[core, jb, 32] = jnp.where(row == 0, mean[:, half], 0.0)
+            put(2 * jb + core, site[:, half], jnp.where(row == 0, mean[:, half], 0.0))
 
 
 class Place:
@@ -109,6 +108,7 @@
         self.xs8 = [8 * v for v in self.xs]
         self.cell_home = 33 + self.home
         self.cell_x8 = 33 + self.x8
+        self.zs2 = [2 * v for v in self.zs]
 
 
 def sum_phases(place, c_ref, o_ref, bufs, send, recv, cells):
@@ -216,6 +216,99 @@
     return [begin, add_core, add_y, add_x, add_z, return_x, return_y, return_core, end]
 
 
+def half_sum_phases(place, c_ref, o_ref, bufs, send, recv):
+    r0, a0, r1, a1, r2, a2, r3 = bufs
+    core, other, y = place.core, place.other, place.y
+    sem = iter(range(COPIES))
+
+    def copy(src, dst, peer):
+        k = next(sem)
+        return lambda: pltpu.make_async_remote_copy(
+            src_ref=src, dst_ref=dst, send_sem=send.at[k], recv_sem=recv.at[k],
+            device_id=peer, device_id_type=MESH,
+        )
+
+    order = (1, 2, 3, 0)
+    to_core = [
+        copy(c_ref.at[other, place.ys[k]], r0.at[place.ys[k]], place.to_core) for k in order
+    ]
+    to_y = [copy(a0.at[place.ys[k]], r1.at[k - 1], place.to_y[k]) for k in range(1, 4)]
+    to_z, back_z = [], []
+    for k in range(1, 8):
+        to_z.append(copy(a1.at[pl.ds(place.zs2[k], 2)], r2.at[k - 1, pl.ds(0, 2)], place.to_z[k]))
+        to_z.append(copy(a1.at[pl.ds(16, 1)], r2.at[k - 1, pl.ds(2, 1)], place.to_z[k]))
+    to_x = [copy(a2, r3.at[k - 1], place.to_x[k]) for k in range(1, 4)]
+    for k in range(1, 8):
+        spot = o_ref.at[core, y, pl.ds(place.zs2[0], 2)]
+        back_z.append(copy(spot, spot, place.to_z[k]))
+    spot = o_ref.at[core, y]
+    back_y = [copy(spot, spot, place.to_y[k]) for k in range(1, 4)]
+    back_core = []
+    for k in range(4):
+        spot = o_ref.at[core, place.ys_back[k]]
+        back_core.append(copy(spot, spot, place.to_core))
+
+    def start(copies):
+        for c in copies:
+            c().start()
+
+    def arrive(copies):
+        for c in copies:
+            c().wait_recv()
+
+    def begin():
+        start(to_core)
+
+    def add_core():
+        for k, c in zip(order, to_core):
+            c().wait_recv()
+            yk = place.ys[k]
+            a0[yk] = c_ref[core, yk] + r0[yk]
+            if k:
+                to_y[k - 1]().start()
+
+    def add_y():
+        arrive(to_y)
+        a1[...] = (a0[y] + r1[0]) + (r1[1] + r1[2])
+        start(to_z)
+
+    def add_z():
+        arrive(to_z)
+        mine = a1[pl.ds(place.zs2[0], 2)]
+        mean = a1[16:17]
+        for k in range(7):
+            mine = mine + r2[k, 0:2]
+            mean = mean + r2[k, 2:3]
+        a2[0:2] = mine
+        a2[2:3] = mean
+        start(to_x)
+
+    def add_x():
+        arrive(to_x)
+        total = (a2[...] + r3[0]) + (r3[1] + r3[2])
+        o_ref[core, y, pl.ds(place.zs2[0], 2)] = total[0:2]
+        o_ref[core, y, 16] = total[2]
+        start(back_z)
+
+    def return_y():
+        arrive(back_z)
+        start(back_y)
+        start(back_core[:1])
+
+    def return_core():
+        for k in range(3):
+            back_y[k]().wait_recv()
+            back_core[k + 1]().start()
+
+    def end():
+        arrive(back_core)
+        for group in (to_core, to_y, to_z, to_x, back_z, back_y, back_core):
+            for c in group:
+                c().wait_send()
+
+    return [begin, add_core, add_y, add_z, add_x, return_y, return_core, end]
+
+
 COPIES = 4 + 3 + 6 + 14 + 14 + 6 + 3 + 4
 
 
@@ -224,6 +317,13 @@
         return pltpu.VMEM(shape + (8, B), F32)
 
     return [buf(4, 33), buf(4, 33), buf(3, 33), buf(33), buf(3, 9), buf(9), buf(7, 2)]
+
+
+def half_sum_buffers():
+    def buf(*shape):
+        return pltpu.VMEM(shape + (8, B), F32)
+
+    return [buf(4, 17), buf(4, 17), buf(3, 17), buf(17), buf(7, 3), buf(3), buf(3, 3)]
 
 
 def factor_block(s, dcol):
@@ -292,7 +392,8 @@
     return jnp.concatenate([line[:, k : k + B] for k in range(0, line.shape[1], B)], axis=0)
 
 
-def analyse(site_of, mean_of, values, variances, damping, x_ref, xm_ref, hooks, between, scratch):
+def analyse(site_of, mean_of, values, variances, damping, x_ref, xm_ref, hooks, between, scratch,
+            late):
     (a_ref, yb_ref, p_ref, qs_ref, s_ref, linv_ref, minv_ref, t1_ref, aq_ref, qv_ref, lz_ref,
      d_ref, var_ref, vcol_ref, gt_ref, k_ref) = scratch
     levels, members, cols = x_ref.shape
@@ -307,11 +408,14 @@
 
     eye_m = jnp.where(square(members), 1.0, 0.0)
     diag = square(B)
-    for i in range(nb):
-        y_i = site_of(i).T
-        a_ref[i * B : (i + 1) * B] = y_i * c
-        yb_ref[i * B : (i + 1) * B] = y_i.astype(BF16)
-        d_ref[i : i + 1] = values[i : i + 1] - mean_of(i)
+    def fill(blocks):
+        for i in blocks:
+            y_i = site_of(i).T
+            a_ref[i * B : (i + 1) * B] = y_i * c
+            yb_ref[i * B : (i + 1) * B] = y_i.astype(BF16)
+            d_ref[i : i + 1] = values[i : i + 1] - mean_of(i)
+
+    fill(range(nb - late))
     var_ref[...] = variances
     var_cols = columns_of(variances)
     for i in range(nb):
@@ -358,6 +462,8 @@
         qv_ref[...] = qv
         for k, hook in enumerate(hooks):
             pl.when(i == k)(hook)
+        if late:
+            pl.when(i == nb - late - 2)(lambda: fill(range(nb - late, nb)))
         return carry
 
     lax.fori_loop(0, nb, step, 0)
@@ -490,8 +596,8 @@
     args, (x_ref, xm_ref), refs = refs[:10], refs[10:12], refs[12:]
     held, refs = refs[:8], refs[8:]
     share0, panel0, share1, panel1, refs = refs[0], refs[1], refs[2], refs[3], refs[4:]
-    bufs0, bufs1, refs = refs[:7], refs[7:14], refs[14:]
-    (load, send0, recv0, send1, recv1), refs = refs[:5], refs[5:]
+    bufs0, bufs2, bufs1, refs = refs[:7], refs[7:14], refs[14:21], refs[21:]
+    (load, send0, recv0, send2, recv2, send1, recv1), refs = refs[:7], refs[7:]
     (yt_ref, ym_ref, cells_ref), scratch = refs[:3], refs[3:]
 
     barrier = pltpu.get_barrier_semaphore()
@@ -510,12 +616,25 @@
     sites = (tile_ref, col_ref, level_ref, frac_ref)
     levels, members, cols = x_ref.shape
 
-    gather_sites(0, True, x_ref, xm_ref, sites, share0)
+    def put_first(i, values, mean):
+        for half in range(2):
+            rows = values[half * B : (half + 1) * B]
+            share0[i // 4, half, i % 4, 0:16] = rows.reshape(16, 8, B)
+            share0[i // 4, half, i % 4, 16] = mean
+
+    def put_second(i, values, mean):
+        share1[i % 2, i // 2, 0:32] = values.reshape(32, 8, B)
+        share1[i % 2, i // 2, 32] = mean
+
+    gather_sites(0, True, (0, 1), x_ref, xm_ref, sites, put_first)
     pl.semaphore_wait(barrier, len(place.peers))
-    first_sum = sum_phases(place, share0, panel0, bufs0, send0, recv0, False)
+    early = half_sum_phases(place, share0.at[0], panel0.at[0], bufs0, send0, recv0)
+    later = half_sum_phases(place, share0.at[1], panel0.at[1], bufs2, send2, recv2)
     second_sum = sum_phases(place, share1, panel1, bufs1, send1, recv1, True)
-    first_sum[0]()
-    gather_sites(1, False, x_ref, xm_ref, sites, share1)
+    early[0]()
+    gather_sites(0, True, (2, 3), x_ref, xm_ref, sites, put_first)
+    later[0]()
+    gather_sites(1, False, range(4), x_ref, xm_ref, sites, put_second)
     r16 = lax.broadcasted_iota(jnp.int32, (B, B), 0)
     own = jnp.zeros((8, B), F32)
     row = lax.broadcasted_iota(jnp.int32, (8, B), 0)
@@ -525,8 +644,11 @@
             own = jnp.where(row == 2 * lev + half, block[0:1], own)
         own = jnp.where(row == 4 + lev, xm_ref[lev : lev + 1, 0:1], own)
     panel1[place.core, place.y, place.cell_home] = own
-    for phase in first_sum[1:]:
-        phase()
+    early[1]()
+    for k in range(2, 7):
+        early[k]()
+        later[k - 1]()
+    early[7]()
     second_sum[0]()
 
     def damping(batch):
@@ -538,18 +660,28 @@
         second_sum[8]()
         update_sites(panel1, lh_ref, lv_ref, sites, scratch, w_lines, yt_ref, ym_ref, cells_ref)
 
+    def both(one, two):
+        def run():
+            one()
+            two()
+        return run
+
     hooks = second_sum[1:7] + [lambda: None, second_sum[7]]
+    hooks[0] = both(later[6], hooks[0])
+    hooks[1] = both(later[7], hooks[1])
     analyse(
-        lambda i: panel0[i % 2, i // 2, 0:32].reshape(members, B),
-        lambda i: panel0[i % 2, i // 2, 32][0:1],
+        lambda i: jnp.concatenate(
+            [panel0[i // 4, half, i % 4, 0:16].reshape(B, B) for half in range(2)], axis=0
+        ),
+        lambda i: panel0[i // 4, 0, i % 4, 16][0:1],
         rows8(val_ref, slice(0, 1)), rows8(var_ref, slice(0, 1)), damping(0), x_ref, xm_ref,
-        hooks, between, scratch,
+        hooks, between, scratch, 4,
     )
     analyse(
         lambda i: yt_ref[:, i * B : (i + 1) * B],
         lambda i: ym_ref[0:1, i * B : (i + 1) * B],
         rows8(val_ref, slice(1, 2)), rows8(var_ref, slice(1, 2)), damping(1), x_ref, xm_ref,
-        [], lambda w_lines: None, scratch,
+        [], lambda w_lines: None, scratch, 0,
     )
 
 
@@ -572,6 +704,7 @@
     n = obs_value.shape[1]
     vm = pl.BlockSpec(memory_space=pltpu.VMEM)
     share = pltpu.VMEM((2, 4, members // 8 + 1, 8, B), F32)
+    halves = pltpu.VMEM((2, 2, 4, members // 16 + 1, 8, B), F32)
     dma = pltpu.SemaphoreType.DMA
     return pl.pallas_call(
         whole_kernel,
@@ -582,10 +715,11 @@
         in_specs=[pl.BlockSpec(memory_space=pltpu.HBM)] * len(args),
         out_specs=(vm, vm),
         scratch_shapes=[pltpu.VMEM(a.shape, a.dtype) for a in args[2:]]
-        + [share, share, share, pltpu.VMEM((2, 4, members // 8 + 33, 8, B), F32)]
+        + [halves, halves, share, pltpu.VMEM((2, 4, members // 8 + 33, 8, B), F32)]
+        + half_sum_buffers()
+        + half_sum_buffers()
         + sum_buffers()
-        + sum_buffers()
-        + [dma((len(args),))] + [dma((COPIES,))] * 4
+        + [dma((len(args),))] + [dma((COPIES,))] * 6
         + [pltpu.VMEM((members, n), F32), pltpu.VMEM((8, n), F32), pltpu.VMEM((members, cols), BF16)]
         + analysis_scratch(n, members, cols),
         compiler_params=pltpu.CompilerParams(

time: 155 us -> 150 us (0.968)
  Pallas kernels: 150 us -> 146 us
    pallas_call x1, Pallas kernels: 150 us -> 146 us  [shards(): pl.pallas_call(whole_kernel, out_shape=(jax.ShapeDtypeStruct(perturb.shap...]
where the time goes in v4:
time: 150 us
  Pallas kernels  146 us (97%)
  local copies, waits for them, and re-layouts  2.47 us (2%)
    pallas_call x1, Pallas kernels, shards(): pl.pallas_call(whole_kernel, out_shape=(jax.ShapeDtypeStruct(perturb.shap...  146 us

profile of v4, /device:TPU:1, one launch (start us, length us, event | category | flops | bytes accessed | tf_op | source)
XLA Modules:
  0.0 149.6 jit_solution(8786489925597317232)
XLA Ops:
  0.6 146.5 %analysis.1 = (bf16[2,256,512]{2,1,0:T(8,128)(2,1)}, f32[2,512]{1,0:T(2,128)}) custom-call(bf16[2,256,512]{2,1,0:T(8,128)(2,1)} %refs_0_.1, f32[2,512]{1,0:T(2,128)} %refs_1_.1, f32[2,1024]{1,0:T(2,128)} %refs_2_.1, f32[2,1024]{1,0:T(2,128)} %refs_3_.1, f32[2,1024]{1,0:T(2,128)} %refs_4_.1, s32[2,1024]{1,0:T(2,128)} %refs_5_.1, s32[2,1024]{1,0:T(2,128)} %refs_6_.1, ...), custom_call_target="tpu_custom_call" | custom-call | tf_op jit(solution)/shard_map/analysis/pallas_call | solution.py:709
  147.1 0.0 copy-start
  147.1 1.9 %copy.14 = bf16[2,256,512]{2,1,0:T(8,128)(2,1)} copy(bf16[2,256,512]{2,1,0:T(8,128)(2,1)} %get-tuple-element.4) | data formatting | bytes 1048576
  149.0 0.0 copy-done
  149.0 0.6 copy.15
Async XLA Ops:
  147.1 1.9 %copy-start = (f32[2,512]{1,0:T(2,128)S(1)}, f32[2,512]{1,0:T(2,128)}, u32[]{:S(2)}) copy-start(f32[2,512]{1,0:T(2,128)} %get-tuple-element.5) | copy-start | bytes 12292

commit v5 on v4

--- a/solution.py
+++ b/solution.py
@@ -394,7 +394,7 @@
 
 def analyse(site_of, mean_of, values, variances, damping, x_ref, xm_ref, hooks, between, scratch,
             late):
-    (a_ref, yb_ref, p_ref, qs_ref, s_ref, linv_ref, minv_ref, t1_ref, aq_ref, qv_ref, lz_ref,
+    (a_ref, yb_ref, p_ref, qs_ref, s_ref, linv_ref, minv_ref, t1_ref, aq_ref, lz_ref,
      d_ref, var_ref, vcol_ref, gt_ref, k_ref) = scratch
     levels, members, cols = x_ref.shape
     n = a_ref.shape[0]
@@ -424,7 +424,7 @@
     qs_ref[0] = eye_m * (1.0 / c)
     a_0 = a_ref[0:B]
     s_ref[...] = mm(a_0, a_0, NT) + jnp.where(diag, var_ref[0:1], 0.0)
-    for ref in (linv_ref, minv_ref, t1_ref, aq_ref, qv_ref):
+    for ref in (linv_ref, minv_ref, t1_ref, aq_ref):
         ref[...] = jnp.zeros_like(ref)
 
     def finish_previous(i):
@@ -435,13 +435,10 @@
         lz_ref[rows_at(i)] = mm(linv, z, TN)
         p = p_ref[...] - mm(v, v, TN)
         q = qs_ref[ip] - mm(v, z, TN)
-        qv = qv_ref[...]
-        rhs = d_ref[pl.ds(ip, 1)] - mm(qv, a_ref[rows_at(ip)], NT)
-        qv = qv + mm(mm(rhs, linv, NT), v)
-        return p, q, qv
+        return p, q
 
     def step(i, carry):
-        p, q, qv = finish_previous(i)
+        p, q = finish_previous(i)
         i_next = jnp.minimum(i + 1, nb - 1)
         a_i = a_ref[rows_at(i)]
         a_n = a_ref[rows_at(i_next)]
@@ -459,7 +456,6 @@
         aq_ref[...] = aq
         p_ref[...] = p
         qs_ref[i] = q
-        qv_ref[...] = qv
         for k, hook in enumerate(hooks):
             pl.when(i == k)(hook)
         if late:
@@ -467,24 +463,37 @@
         return carry
 
     lax.fori_loop(0, nb, step, 0)
-    p, q, qv = finish_previous(nb)
-
-    def over_obs(rows):
-        total = jnp.zeros((8, members), F32)
+    p, q = finish_previous(nb)
+
+    d_cols = columns_of(d_ref[...])
+    inv_var = [1.0 / vcol_ref[i] for i in range(nb)]
+
+    def over_obs(lines):
+        total = 0.0
         for i in range(nb):
-            total = total + mm(jnp.broadcast_to(rows[i : i + 1], (8, B)), a_ref[i * B : (i + 1) * B])
-        return total
+            part = a_ref[i * B : (i + 1) * B] * lines[i]
+            total = total + jnp.sum(part.reshape(B // 8, 8, members), axis=0)
+        return jnp.sum(total, axis=0, keepdims=True)
 
     def times_a(v):
-        return jnp.concatenate(
-            [mm(v, a_ref[i * B : (i + 1) * B], NT)[0:1] for i in range(nb)], axis=0
-        )
-
-    d, var = d_ref[...], var_ref[...]
-    w = (d - times_a(qv)) / var
-    rest = d - var * w - times_a(over_obs(w))
-    w = w + (rest - times_a(mm(over_obs(rest / var), p))) / var
-    w_cols = columns_of(w)
+        return [
+            jnp.sum(a_ref[i * B : (i + 1) * B] * v, axis=1, keepdims=True) for i in range(nb)
+        ]
+
+    def solve_for(rest):
+        v = over_obs([r * inv[:, 0:1] for r, inv in zip(rest, inv_var)])
+        back = times_a(mm(jnp.broadcast_to(v, (8, members)), p)[0:1])
+        return [(r - t) * inv[:, 0:1] for r, t, inv in zip(rest, back, inv_var)]
+
+    d_lines = [d_cols[:, i : i + 1] for i in range(nb)]
+    w_lines = solve_for(d_lines)
+    for _ in range(1):
+        back = times_a(over_obs(w_lines))
+        rest = [
+            d - vcol_ref[i][:, 0:1] * w - t
+            for i, (d, w, t) in enumerate(zip(d_lines, w_lines, back))
+        ]
+        w_lines = [w + more for w, more in zip(w_lines, solve_for(rest))]
 
     for i in range(nb):
         g = lz_ref[(i + 1) * B : (i + 2) * B]
@@ -493,7 +502,6 @@
             g = g - mm(a_ref[i * B : (i + 1) * B], qs_ref[i + 1] - q) * jnp.concatenate([inv, inv], 1)
         gt_ref[:, i * B : (i + 1) * B] = g.T.astype(BF16)
 
-    w_lines = [w_cols[:, i : i + 1] for i in range(nb)]
     between(w_lines)
     for lev in range(levels):
         damp_cols = columns_of(damping[lev] * (1.0 / (members - 1.0)))
@@ -529,7 +537,7 @@
 
 def update_sites(share_ref, lh_ref, lv_ref, sites, scratch, w_lines, yt_ref, ym_ref, cells_ref):
     tile_ref, col_ref, level_ref, frac_ref = sites
-    yb_ref, gt_ref, k_ref = scratch[1], scratch[14], scratch[15]
+    yb_ref, gt_ref, k_ref = scratch[1], scratch[13], scratch[14]
     n, members = yb_ref.shape
     cols = k_ref.shape[1]
     tiles, levels = lh_ref.shape[1], lv_ref.shape[1]
@@ -693,7 +701,7 @@
 
     return [
         buf(n, e), pltpu.VMEM((n, e), BF16), buf(e, e), buf(nb + 1, e, e), buf(B, B), buf(B, B),
-        buf(B, B), buf(B, e), buf(B, e), buf(8, e), buf(n + B, e), buf(nb, B), buf(nb, B),
+        buf(B, B), buf(B, e), buf(B, e), buf(n + B, e), buf(nb, B), buf(nb, B),
         buf(nb, B, B), pltpu.VMEM((e, n), BF16), pltpu.VMEM((n, cols), BF16),
     ]
 

time: 150 us -> 140 us (0.933)
  Pallas kernels: 146 us -> 136 us
    pallas_call x1, Pallas kernels: 146 us -> 136 us  [shards(): pl.pallas_call(whole_kernel, out_shape=(jax.ShapeDtypeStruct(perturb.shap...]
where the time goes in v5:
time: 140 us; the launch traced here: 139 us
  Pallas kernels  136 us (97%)
  local copies, waits for them, and re-layouts  2.47 us (2%)
    pallas_call x1, Pallas kernels, shards(): pl.pallas_call(whole_kernel, out_shape=(jax.ShapeDtypeStruct(perturb.shap...  136 us

profile of v5, /device:TPU:1, one launch (start us, length us, event | category | flops | bytes accessed | tf_op | source)
XLA Modules:
  0.0 139.5 jit_solution(1767794013364379910)
XLA Ops:
  0.6 136.4 %analysis.1 = (bf16[2,256,512]{2,1,0:T(8,128)(2,1)}, f32[2,512]{1,0:T(2,128)}) custom-call(bf16[2,256,512]{2,1,0:T(8,128)(2,1)} %refs_0_.1, f32[2,512]{1,0:T(2,128)} %refs_1_.1, f32[2,1024]{1,0:T(2,128)} %refs_2_.1, f32[2,1024]{1,0:T(2,128)} %refs_3_.1, f32[2,1024]{1,0:T(2,128)} %refs_4_.1, s32[2,1024]{1,0:T(2,128)} %refs_5_.1, s32[2,1024]{1,0:T(2,128)} %refs_6_.1, ...), custom_call_target="tpu_custom_call" | custom-call | tf_op jit(solution)/shard_map/analysis/pallas_call | solution.py:717
  137.0 0.0 copy-start
  137.0 1.9 %copy.14 = bf16[2,256,512]{2,1,0:T(8,128)(2,1)} copy(bf16[2,256,512]{2,1,0:T(8,128)(2,1)} %get-tuple-element.4) | data formatting | bytes 1048576
  138.9 0.0 copy-done
  138.9 0.6 copy.15
Async XLA Ops:
  137.0 1.9 %copy-start = (f32[2,512]{1,0:T(2,128)S(1)}, f32[2,512]{1,0:T(2,128)}, u32[]{:S(2)}) copy-start(f32[2,512]{1,0:T(2,128)} %get-tuple-element.5) | copy-start | bytes 12292

commit v6 on v5

--- a/solution.py
+++ b/solution.py
@@ -642,6 +642,7 @@
     early[0]()
     gather_sites(0, True, (2, 3), x_ref, xm_ref, sites, put_first)
     later[0]()
+    early[1]()
     gather_sites(1, False, range(4), x_ref, xm_ref, sites, put_second)
     r16 = lax.broadcasted_iota(jnp.int32, (B, B), 0)
     own = jnp.zeros((8, B), F32)
@@ -652,7 +653,6 @@
             own = jnp.where(row == 2 * lev + half, block[0:1], own)
         own = jnp.where(row == 4 + lev, xm_ref[lev : lev + 1, 0:1], own)
     panel1[place.core, place.y, place.cell_home] = own
-    early[1]()
     for k in range(2, 7):
         early[k]()
         later[k - 1]()

time: 140 us -> 138 us (0.986)
    pallas_call x1, Pallas kernels: 136 us -> 135 us  [shards(): pl.pallas_call(whole_kernel, out_shape=(jax.ShapeDtypeStruct(perturb.shap...]
where the time goes in v6:
time: 138 us
  Pallas kernels  135 us (98%)
  local copies, waits for them, and re-layouts  2.47 us (2%)
    pallas_call x1, Pallas kernels, shards(): pl.pallas_call(whole_kernel, out_shape=(jax.ShapeDtypeStruct(perturb.shap...  135 us

profile of v6, /device:TPU:1, one launch (start us, length us, event | category | flops | bytes accessed | tf_op | source)
XLA Modules:
  0.0 137.7 jit_solution(5897782656386919618)
XLA Ops:
  0.6 134.6 %analysis.1 = (bf16[2,256,512]{2,1,0:T(8,128)(2,1)}, f32[2,512]{1,0:T(2,128)}) custom-call(bf16[2,256,512]{2,1,0:T(8,128)(2,1)} %refs_0_.1, f32[2,512]{1,0:T(2,128)} %refs_1_.1, f32[2,1024]{1,0:T(2,128)} %refs_2_.1, f32[2,1024]{1,0:T(2,128)} %refs_3_.1, f32[2,1024]{1,0:T(2,128)} %refs_4_.1, s32[2,1024]{1,0:T(2,128)} %refs_5_.1, s32[2,1024]{1,0:T(2,128)} %refs_6_.1, ...), custom_call_target="tpu_custom_call" | custom-call | tf_op jit(solution)/shard_map/analysis/pallas_call | solution.py:717
  135.3 0.0 copy-start
  135.3 1.9 %copy.14 = bf16[2,256,512]{2,1,0:T(8,128)(2,1)} copy(bf16[2,256,512]{2,1,0:T(8,128)(2,1)} %get-tuple-element.4) | data formatting | bytes 1048576
  137.1 0.0 copy-done
  137.1 0.6 copy.15
Async XLA Ops:
  135.3 1.9 %copy-start = (f32[2,512]{1,0:T(2,128)S(1)}, f32[2,512]{1,0:T(2,128)}, u32[]{:S(2)}) copy-start(f32[2,512]{1,0:T(2,128)} %get-tuple-element.5) | copy-start | bytes 12292
